TPU v7x, 32 devices: a whole 2x2x4 slice. The times are simulated.
32 devices in a mesh: tm: 4 (over x, core), height: 2 (over y), fsdp: 4 (over z).
Axes of the slice: x: 2, y: 2, z: 4, core: 2. Of those that a mesh axis runs over, the one named last changes fastest.
Arguments:
- query_primal: bfloat16 [4, 16, 8, 8, 1536], P('fsdp', 'tm', 'height'), may hold values from -125 to 125
- key_primal: bfloat16 [4, 16, 8, 8, 1536], P('fsdp', 'tm', 'height'), may hold values from -5 to 5
- value_primal: bfloat16 [4, 16, 8, 8, 1536], P('fsdp', 'tm', 'height'), may hold values from -6 to 6
- query_tangent: bfloat16 [4, 16, 8, 8, 1536], P('fsdp', 'tm', 'height'), may hold values from -6 to 6
- key_tangent: bfloat16 [4, 16, 8, 8, 1536], P('fsdp', 'tm', 'height'), may hold values from -6 to 6
- value_tangent: bfloat16 [4, 16, 8, 8, 1536], P('fsdp', 'tm', 'height'), may hold values from -6 to 6
- out_weight: bfloat16 [1536, 1536], P(None, ('height', 'fsdp')), may hold values from -0.15625 to 0.15625
- gate_table: float32 [64, 1536], replicated, may hold values from 0.5 to 1.5
- gate_slope: float32 [64, 1536], replicated, may hold values from -4 to 4
- timestep: int32 [4], P('fsdp'), may hold values from 0 to 63
Outputs:
- output_primal: bfloat16 [4, 16, 8, 8, 1536], P('fsdp', 'tm', 'height')
- output_tangent: bfloat16 [4, 16, 8, 8, 1536], P('fsdp', 'tm', 'height')
All inputs are finite; a program needn't handle non-finite values.
Results may differ from a plain program's by a relative error of at most 0.008.
Values may be sent and summed in bfloat16 or wider, within the bound.
No kernel may reach another device: no remote copies, remote signals or barrier semaphores. Data moves between devices by JAX's collectives and lax.ppermute only.
A program may use at most 64 MiB of HBM per device.

v0:
```python
import math

import jax
import jax.numpy as jnp
from jax import lax
from jax.sharding import PartitionSpec as P

HD = 128


def partner_2(value, axis, apart):
    mask = 2**apart
    pairs = [(source, source ^ mask) for source in range(lax.axis_size(axis))]
    return lax.ppermute(value, axis, pairs)


def with_halo(x, sides, width):
    for axis, dim in sides:
        devices, length = (lax.axis_size(axis), x.shape[dim])
        up = [(i, (i + 1) % devices) for i in range(devices - 1)]
        down = [(j, i) for i, j in up]
        last = lax.slice_in_dim(x, length - width, length, axis=dim)
        first = lax.slice_in_dim(x, 0, width, axis=dim)
        before = lax.ppermute(last, axis, up)
        after = lax.ppermute(first, axis, down)
        x = jnp.concatenate([before, x, after], axis=dim)
    return x


def attend(queries, keys_all, values_all, queries_t, keys_t, values_t, allowed):
    scaling = 1.0 / math.sqrt(queries.shape[-1])
    scores = (
        jnp.einsum("qhd,khd->hqk", queries, keys_all, preferred_element_type=jnp.float32) * scaling
    )
    scores = jnp.where(allowed[None], scores, -1e30)
    row_max = jnp.max(scores, axis=-1, keepdims=True)
    lifted = jnp.exp(scores - row_max)
    probs = lifted / jnp.sum(lifted, axis=-1, keepdims=True)
    probs_low = probs.astype(jnp.bfloat16)
    primal = jnp.einsum("hqk,khd->qhd", probs_low, values_all, preferred_element_type=jnp.float32)
    joined_q = jnp.concatenate([queries_t, queries], 2)
    joined_k = jnp.concatenate([keys_all, keys_t], 2)
    slopes = (
        jnp.einsum("qhd,khd->hqk", joined_q, joined_k, preferred_element_type=jnp.float32) * scaling
    )
    centre = jnp.sum(probs * slopes, axis=-1, keepdims=True)
    weights_t = (probs * (slopes - centre)).astype(jnp.bfloat16)
    joined_w = jnp.concatenate([weights_t, probs_low], 2)
    joined_v = jnp.concatenate([values_all, values_t], 0)
    tangent = jnp.einsum("hqk,khd->qhd", joined_w, joined_v, preferred_element_type=jnp.float32)
    return (primal.astype(jnp.bfloat16), tangent.astype(jnp.bfloat16))


def finish(stacked, weight_block, gate_part, slope_part):
    pair_count, token_count, features = stacked.shape
    both = jnp.dot(
        stacked.reshape(pair_count * token_count, features),
        weight_block,
        preferred_element_type=jnp.float32,
    ).reshape(pair_count, token_count, -1)
    out_p = (gate_part * both[0]).astype(jnp.bfloat16)
    out_t = (gate_part * both[1] + slope_part * both[0]).astype(jnp.bfloat16)
    return jnp.stack([out_p, out_t])


def local(
    query_primal,
    key_primal,
    value_primal,
    query_tangent,
    key_tangent,
    value_tangent,
    out_weight,
    gate_table,
    gate_slope,
    timestep,
):
    frames_dev = query_primal.shape[1]
    rows_dev = query_primal.shape[2]
    columns = query_primal.shape[3]
    features = query_primal.shape[4]
    head_count = features // HD
    packed = jnp.stack([key_primal, value_primal, key_tangent, value_tangent])[:, 0]
    partner = partner_2(packed, "height", 0)
    lower_half = lax.axis_index("height") % 2 == 0
    tile_block = jnp.where(
        lower_half, jnp.concatenate([packed, partner], 2), jnp.concatenate([partner, packed], 2)
    )
    extended = with_halo(tile_block, (("tm", 1),), 1)
    ext_frames = frames_dev + 2
    key_sets = extended.reshape(4, -1, head_count, HD)
    frame_ids = lax.broadcasted_iota(jnp.int32, (ext_frames, 2 * rows_dev, columns), 0).reshape(-1)
    global_frame = lax.axis_index("tm") * frames_dev + frame_ids - 1
    total_frames = frames_dev * lax.axis_size("tm")
    inside = (global_frame >= 0) & (global_frame < total_frames)
    allowed = inside[None, :]
    query_flat = query_primal.reshape(-1, head_count, HD)
    query_flat_t = query_tangent.reshape(-1, head_count, HD)
    primal, tangent = attend(
        query_flat, key_sets[0], key_sets[1], query_flat_t, key_sets[2], key_sets[3], allowed
    )
    token_count = query_flat.shape[0]
    stacked = jnp.stack(
        [primal.reshape(token_count, features), tangent.reshape(token_count, features)]
    )
    step_total = gate_table.shape[0]
    chosen = lax.broadcasted_iota(jnp.int32, (step_total, 1), 0) == timestep[0]
    gate_row = jnp.sum(jnp.where(chosen, gate_table, 0.0), axis=0)
    slope_row = jnp.sum(jnp.where(chosen, gate_slope, 0.0), axis=0)
    result = finish(
        stacked,
        lax.all_gather(out_weight, ("height", "fsdp"), axis=1, tiled=True),
        gate_row,
        slope_row,
    )
    dout = result.shape[2]
    out_p = result[0].reshape(1, frames_dev, rows_dev, columns, dout)
    out_t = result[1].reshape(1, frames_dev, rows_dev, columns, dout)
    return (out_p, out_t)


def solution(mesh):
    in_specs = (
        P("fsdp", "tm", "height", None, None),
        P("fsdp", "tm", "height", None, None),
        P("fsdp", "tm", "height", None, None),
        P("fsdp", "tm", "height", None, None),
        P("fsdp", "tm", "height", None, None),
        P("fsdp", "tm", "height", None, None),
        P(None, ("height", "fsdp")),
        P(),
        P(),
        P("fsdp"),
    )
    out_specs = (P("fsdp", "tm", "height", None, None), P("fsdp", "tm", "height", None, None))
    return jax.shard_map(local, mesh=mesh, in_specs=in_specs, out_specs=out_specs, check_vma=False)
```

profile of v0, /device:TPU:1, one launch (start us, length us, event | category | flops | bytes accessed | tf_op | source)
XLA Modules:
  0.0 116.4 jit_solution(643211712569957955)
XLA Ops:
  7.9 1.5 %maximum_bitcast_fusion = bf16[4,4,4,8,1536]{4,3,2,1,0:T(8,128)(2,1)S(1)} fusion(bf16[1,1,4,4,8,1536]{5,4,3,2,1,0:T(8,128)(2,1)} %bitcast.50, bf16[1,1,4,4,8,1536]{5,4,3,2,1,0:T(8,128)(2,1)} %bitcast.51, bf16[1,1,4,4,8,1536]{5,4,3,2,1,0:T(8,128)(2,1)} %bitcast.52, bf16[1,1,4,4,8,1536]{5,4,3,2,1,0:T(8,128)(2,1)} %bitcast.53), kind=kLoop, calls=%fused_computation.24 | loop fusion | flops 2359296 | bytes 3145728 | tf_op jit(solution)/shard_map/squeeze | solution.py:83
  9.5 2.1 %collective-permute-start = (bf16[4,4,4,8,1536]{4,3,2,1,0:T(8,128)(2,1)S(1)}, bf16[4,4,4,8,1536]{4,3,2,1,0:T(8,128)(2,1)}, u32[]{:S(2)}, u32[]{:S(2)}) collective-permute-start(bf16[4,4,4,8,1536]{4,3,2,1,0:T(8,128)(2,1)S(1)} %maximum_bitcast_fusion), channel_id=1, source_target_pairs={{0,4},{4,0},{1,5},{5,1},{2,6},{6,2},{3,7},{7,3},{8,12},{12,8},{9,1... | collective-permute-start | bytes 4718600 | tf_op jit(solution)/shard_map/ppermute | solution.py:14
  11.6 40.5 %collective-permute-done = bf16[4,4,4,8,1536]{4,3,2,1,0:T(8,128)(2,1)} collective-permute-done((bf16[4,4,4,8,1536]{4,3,2,1,0:T(8,128)(2,1)S(1)}, bf16[4,4,4,8,1536]{4,3,2,1,0:T(8,128)(2,1)}, u32[]{:S(2)}, u32[]{:S(2)}) %collective-permute-start) | collective-permute-done | bytes 1572896 | tf_op jit(solution)/shard_map/ppermute | solution.py:14
  52.1 3.4 %maximum_select_fusion = bf16[4,4,8,8,1536]{4,3,2,1,0:T(8,128)(2,1)S(1)} fusion(bf16[4,4,4,8,1536]{4,3,2,1,0:T(8,128)(2,1)} %collective-permute-done, bf16[4,4,4,8,1536]{4,3,2,1,0:T(8,128)(2,1)} %copy-done, pred[]{:T(512)S(6)} %eq.18), kind=kLoop, calls=%fused_computation.3 | loop fusion | flops 4718592 | bytes 6291457 | tf_op jit(solution)/shard_map/jit(_where)/select_n | solution.py:86
  55.5 1.3 %fusion.47 = (bf16[4,1,8,8,1536]{4,3,2,1,0:T(8,128)(2,1)}, bf16[4,1,8,8,1536]{4,3,2,1,0:T(8,128)(2,1)}) fusion(bf16[4,4,8,8,1536]{4,3,2,1,0:T(8,128)(2,1)S(1)} %maximum_select_fusion), kind=kLoop, calls=%fused_computation.55 | loop fusion | bytes 3145728 | tf_op jit(solution)/shard_map/slice | solution.py:22
  56.9 3.3 %collective-permute-start.2 = (bf16[4,1,8,8,1536]{4,3,2,1,0:T(8,128)(2,1)}, bf16[4,1,8,8,1536]{4,3,2,1,0:T(8,128)(2,1)}, u32[]{:S(2)}, u32[]{:S(2)}) collective-permute-start(bf16[4,1,8,8,1536]{4,3,2,1,0:T(8,128)(2,1)} %get-tuple-element.9), channel_id=1, source_target_pairs={{8,0},{16,8},{24,16},{9,1},{17,9},{25,17},{10,2},{18,10},{26,18},{... | collective-permute-start | bytes 2359304 | tf_op jit(solution)/shard_map/ppermute | solution.py:25
  60.2 3.0 %collective-permute-start.1 = (bf16[4,1,8,8,1536]{4,3,2,1,0:T(8,128)(2,1)}, bf16[4,1,8,8,1536]{4,3,2,1,0:T(8,128)(2,1)}, u32[]{:S(2)}, u32[]{:S(2)}) collective-permute-start(bf16[4,1,8,8,1536]{4,3,2,1,0:T(8,128)(2,1)} %get-tuple-element.8), channel_id=1, source_target_pairs={{0,8},{8,16},{16,24},{1,9},{9,17},{17,25},{2,10},{10,18},{18,26},{... | collective-permute-start | bytes 2359304 | tf_op jit(solution)/shard_map/ppermute | solution.py:24
  66.2 2.3 %reshape.57 = bf16[128,12,128]{2,1,0:T(8,128)(2,1)} reshape(bf16[1,4,4,8,1536]{4,3,2,1,0:T(8,128)(2,1)} %param.13) | data formatting | bytes 786432 | tf_op jit(solution)/shard_map/reshape | solution.py:98
  68.4 1.9 %copy.23 = bf16[128,12,128]{2,0,1:T(8,128)(2,1)} copy(bf16[128,12,128]{2,1,0:T(8,128)(2,1)} %reshape.57) | data formatting | bytes 786432 | tf_op jit(solution)/shard_map/reshape | solution.py:98
  71.0 1.3 %select_reduce_fusion = (f32[1536]{0:T(1024)S(1)}, f32[1536]{0:T(1024)S(1)}) fusion(f32[64,1536]{1,0:T(8,128)} %param.18, pred[64]{0:T(512)(128)(4,1)S(1)} %iota_compare_fusion, f32[64,1536]{1,0:T(8,128)} %param.17), kind=kLoop, calls=%fused_computation.40 | loop fusion | flops 390144 | bytes 798784 | tf_op jit(solution)/shard_map/reduce_sum | solution.py:109
  72.5 1.7 %pad_maximum_fusion = bf16[4,6,8,8,1536]{4,3,2,1,0:T(8,128)(2,1)S(1)} fusion(bf16[4,1,8,8,1536]{4,3,2,1,0:T(8,128)(2,1)} %collective-permute-done.2, bf16[4,4,8,8,1536]{4,3,2,1,0:T(8,128)(2,1)S(1)} %maximum_select_fusion, bf16[4,1,8,8,1536]{4,3,2,1,0:T(8,128)(2,1)} %collective-permute-done.1), kind=kLoop, calls=%fused_computation.2 | loop fusion | flops 4718592 | bytes 9437184 | tf_op jit(solution)/shard_map/concatenate | solution.py:26
  74.2 1.9 %fusion.46 = (bf16[1,6,8,8,1536]{4,3,2,1,0:T(8,128)(2,1)S(1)}, bf16[1,6,8,8,1536]{4,3,2,1,0:T(8,128)(2,1)}, bf16[1,6,8,8,1536]{4,3,2,1,0:T(8,128)(2,1)}, bf16[1,6,8,8,1536]{4,3,2,1,0:T(8,128)(2,1)}) fusion(bf16[4,6,8,8,1536]{4,3,2,1,0:T(8,128)(2,1)S(1)} %pad_maximum_fusion), kind=kLoop, calls=%fused_computation.54 | loop fusion | bytes 9437184 | tf_op jit(solution)/shard_map/slice | solution.py:100
  76.1 2.5 %squeeze.24 = bf16[384,12,128]{2,1,0:T(8,128)(2,1)S(1)} reshape(bf16[1,6,8,8,1536]{4,3,2,1,0:T(8,128)(2,1)} %get-tuple-element.7) | data formatting | bytes 2359296 | tf_op jit(solution)/shard_map/squeeze | solution.py:100
  78.6 1.4 %copy.17 = bf16[384,12,128]{2,0,1:T(8,128)(2,1)} copy(bf16[384,12,128]{2,1,0:T(8,128)(2,1)S(1)} %squeeze.24) | data formatting | bytes 2359296 | tf_op jit(solution)/shard_map/squeeze | solution.py:100
  80.0 2.5 %squeeze.26 = bf16[384,12,128]{2,1,0:T(8,128)(2,1)S(1)} reshape(bf16[1,6,8,8,1536]{4,3,2,1,0:T(8,128)(2,1)} %get-tuple-element.5) | data formatting | bytes 2359296 | tf_op jit(solution)/shard_map/squeeze | solution.py:100
  82.5 1.3 %copy.26 = bf16[384,12,128]{2,0,1:T(8,128)(2,1)} copy(bf16[384,12,128]{2,1,0:T(8,128)(2,1)S(1)} %squeeze.26) | data formatting | bytes 2359296 | tf_op jit(solution)/shard_map/squeeze | solution.py:100
  83.9 2.5 %squeeze.25 = bf16[384,12,128]{2,1,0:T(8,128)(2,1)S(1)} reshape(bf16[1,6,8,8,1536]{4,3,2,1,0:T(8,128)(2,1)} %get-tuple-element.6) | data formatting | bytes 2359296 | tf_op jit(solution)/shard_map/squeeze | solution.py:100
  86.4 1.9 %copy.22 = bf16[384,12,128]{0,2,1:T(8,128)(2,1)} copy(bf16[384,12,128]{2,1,0:T(8,128)(2,1)S(1)} %squeeze.25) | data formatting | bytes 2359296 | tf_op jit(solution)/shard_map/squeeze | solution.py:100
  89.1 1.9 %copy.19 = bf16[384,12,128]{0,2,1:T(8,128)(2,1)} copy(bf16[384,12,128]{2,1,0:T(8,128)(2,1)S(1)} %squeeze.23) | data formatting | bytes 2359296 | tf_op jit(solution)/shard_map/squeeze | solution.py:100
  91.0 3.5 %fusion.6 = f32[12,128,384]{1,2,0:T(8,128)} fusion(bf16[384,12,128]{2,0,1:T(8,128)(2,1)} %copy.26, bf16[384,12,128]{2,0,1:T(8,128)(2,1)S(1)} %copy-done.3, bf16[128,12,128]{2,0,1:T(8,128)(2,1)S(1)} %copy.18, bf16[128,12,128]{2,0,1:T(8,128)(2,1)S(1)} %copy-done.7), kind=kOutput, calls=%fused_computation.8 | convolution fusion | flops 308281344 | bytes 5505024 | tf_op jit(solution)/shard_map/qhd,khd->hqk/dot_general | solution.py:44
  94.5 2.5 %fusion.48 = (f32[12,128]{1,0:T(8,128)}, f32[12,128,384]{1,2,0:T(8,128)S(1)}) fusion(pred[384]{0:T(512)(128)(4,1)} %and.19, bf16[384,12,128]{2,0,1:T(8,128)(2,1)S(1)} %copy-done.3, bf16[128,12,128]{2,0,1:T(8,128)(2,1)} %copy-done.6), kind=kOutput, calls=%fused_computation.56 | convolution fusion | flops 153354624 | bytes 3938688 | tf_op jit(solution)/shard_map/sub | solution.py:37
  97.0 1.5 %copy-done.2 = f32[12,128,384]{1,2,0:T(8,128)} copy-done((f32[12,128,384]{1,2,0:T(8,128)}, f32[12,128,384]{1,2,0:T(8,128)S(1)}, u32[]{:S(2)}) %copy-start.2) | copy-done | bytes 2359320
  99.6 3.4 %multiply_convert_fusion = bf16[12,128,384]{1,2,0:T(8,128)(2,1)S(1)} fusion(f32[12,128,384]{1,2,0:T(8,128)S(1)} %copy-done.9, f32[12,128,384]{1,2,0:T(8,128)} %copy-done.2, f32[12,128]{1,0:T(8,128)S(1)} %copy-done.8), kind=kOutput, calls=%fused_computation.19 | output fusion | flops 4720511 | bytes 5904384 | tf_op jit(solution)/shard_map/sub | solution.py:47
  104.8 3.7 %fusion.49 = f32[256,1536]{1,0:T(8,128)S(1)} fusion(bf16[256,1536]{1,0:T(8,128)(2,1)S(1)} %bitcast.49, bf16[1536,1536]{0,1:T(8,128)(2,1)} %all-gather.2.cloned.1.call-done), kind=kOutput, calls=%fused_computation.57 | convolution fusion | flops 1207959552 | bytes 7077888 | tf_op jit(solution)/shard_map/dot_general | solution.py:56
  (37 shorter events, 8.5 us)
Async XLA Ops:
  7.2 97.6 %all-gather.2.cloned.1.call-start = ((), (), s32[]{:S(2)}) async-start(), calls=%async_computation | async-start | bytes 5308416 | tf_op jit(solution)/shard_map/all_gather | solution.py:112
  9.5 2.1 %copy-start = (bf16[4,4,4,8,1536]{4,3,2,1,0:T(8,128)(2,1)}, bf16[4,4,4,8,1536]{4,3,2,1,0:T(8,128)(2,1)S(1)}, u32[]{:S(2)}) copy-start(bf16[4,4,4,8,1536]{4,3,2,1,0:T(8,128)(2,1)S(1)} %maximum_bitcast_fusion) | copy-start | bytes 4718596
  9.5 42.7 %collective-permute-start = (bf16[4,4,4,8,1536]{4,3,2,1,0:T(8,128)(2,1)S(1)}, bf16[4,4,4,8,1536]{4,3,2,1,0:T(8,128)(2,1)}, u32[]{:S(2)}, u32[]{:S(2)}) collective-permute-start(bf16[4,4,4,8,1536]{4,3,2,1,0:T(8,128)(2,1)S(1)} %maximum_bitcast_fusion), channel_id=1, source_target_pairs={{0,4},{4,0},{1,5},{5,1},{2,6},{6,2},{3,7},{7,3},{8,12},{12,8},{9,1... | collective-permute-start | bytes 4718600 | tf_op jit(solution)/shard_map/ppermute | solution.py:14
  55.5 8.4 %copy-start.5 = (bf16[1,4,4,8,1536]{4,3,2,1,0:T(8,128)(2,1)S(1)}, bf16[1,4,4,8,1536]{4,3,2,1,0:T(8,128)(2,1)}, u32[]{:S(2)}) copy-start(bf16[1,4,4,8,1536]{4,3,2,1,0:T(8,128)(2,1)} %param.10) | copy-start | bytes 1179652
  56.9 15.4 %collective-permute-start.2 = (bf16[4,1,8,8,1536]{4,3,2,1,0:T(8,128)(2,1)}, bf16[4,1,8,8,1536]{4,3,2,1,0:T(8,128)(2,1)}, u32[]{:S(2)}, u32[]{:S(2)}) collective-permute-start(bf16[4,1,8,8,1536]{4,3,2,1,0:T(8,128)(2,1)} %get-tuple-element.9), channel_id=1, source_target_pairs={{8,0},{16,8},{24,16},{9,1},{17,9},{25,17},{10,2},{18,10},{26,18},{... | collective-permute-start | bytes 2359304 | tf_op jit(solution)/shard_map/ppermute | solution.py:25
  60.2 12.3 %collective-permute-start.1 = (bf16[4,1,8,8,1536]{4,3,2,1,0:T(8,128)(2,1)}, bf16[4,1,8,8,1536]{4,3,2,1,0:T(8,128)(2,1)}, u32[]{:S(2)}, u32[]{:S(2)}) collective-permute-start(bf16[4,1,8,8,1536]{4,3,2,1,0:T(8,128)(2,1)} %get-tuple-element.8), channel_id=1, source_target_pairs={{0,8},{8,16},{16,24},{1,9},{9,17},{17,25},{2,10},{10,18},{18,26},{... | collective-permute-start | bytes 2359304 | tf_op jit(solution)/shard_map/ppermute | solution.py:24
  66.2 24.9 %copy-start.6 = (bf16[128,12,128]{2,0,1:T(8,128)(2,1)}, bf16[128,12,128]{2,0,1:T(8,128)(2,1)S(1)}, u32[]{:S(2)}) copy-start(bf16[128,12,128]{2,0,1:T(8,128)(2,1)S(1)} %copy.18) | copy-start | bytes 1179652
  88.3 2.8 %copy-start.7 = (bf16[128,12,128]{2,0,1:T(8,128)(2,1)S(1)}, bf16[128,12,128]{2,0,1:T(8,128)(2,1)}, u32[]{:S(2)}) copy-start(bf16[128,12,128]{2,0,1:T(8,128)(2,1)} %copy.23) | copy-start | bytes 1179652
  89.1 1.9 %copy-start.3 = (bf16[384,12,128]{2,0,1:T(8,128)(2,1)S(1)}, bf16[384,12,128]{2,0,1:T(8,128)(2,1)}, u32[]{:S(2)}) copy-start(bf16[384,12,128]{2,0,1:T(8,128)(2,1)} %copy.17) | copy-start | bytes 3538948
  97.0 1.5 %copy-start.2 = (f32[12,128,384]{1,2,0:T(8,128)}, f32[12,128,384]{1,2,0:T(8,128)S(1)}, u32[]{:S(2)}) copy-start(f32[12,128,384]{1,2,0:T(8,128)S(1)} %get-tuple-element.13) | copy-start | bytes 7077892
  97.0 2.5 %copy-start.8 = (f32[12,128]{1,0:T(8,128)S(1)}, f32[12,128]{1,0:T(8,128)}, u32[]{:S(2)}) copy-start(f32[12,128]{1,0:T(8,128)} %get-tuple-element.12) | copy-start | bytes 18436
  97.0 2.5 %copy-start.9 = (f32[12,128,384]{1,2,0:T(8,128)S(1)}, f32[12,128,384]{1,2,0:T(8,128)}, u32[]{:S(2)}) copy-start(f32[12,128,384]{1,2,0:T(8,128)} %fusion.6) | copy-start | bytes 7077892
  99.5 3.4 %copy-start.1 = (bf16[384,12,128]{0,2,1:T(8,128)(2,1)S(1)}, bf16[384,12,128]{0,2,1:T(8,128)(2,1)}, u32[]{:S(2)}) copy-start(bf16[384,12,128]{0,2,1:T(8,128)(2,1)} %copy.19) | copy-start | bytes 3538948
  99.6 3.4 %copy-start.4 = (bf16[384,12,128]{0,2,1:T(8,128)(2,1)S(1)}, bf16[384,12,128]{0,2,1:T(8,128)(2,1)}, u32[]{:S(2)}) copy-start(bf16[384,12,128]{0,2,1:T(8,128)(2,1)} %copy.22) | copy-start | bytes 3538948
Sparse Core Ops, SparseCore 0:
  10.1 84.2 all-gather.1
where the time goes:
time: 118 us; the launch traced here: 116 us
  waiting for transfers between devices  41.5 us (35%)
  local copies, waits for them, and re-layouts  27 us (23%)
  between operations  14.9 us (13%)
  other arithmetic  13.5 us (11%)
  matrix products  11 us (9%)
  starting transfers between devices  8.53 us (7%)
    ppermute x1, waiting for transfers between devices, partner_2(): return lax.ppermute(value, axis, pairs)  40.5 us
    squeeze x2, local copies, waits for them, and re-layouts, local(): key_sets[3]  4.39 us
    reshape x2, local copies, waits for them, and re-layouts, local(): query_flat_t = query_tangent.reshape(-1, head_count, HD)  4.15 us
    squeeze x2, local copies, waits for them, and re-layouts, local(): key_sets[0]  3.89 us
    squeeze x2, local copies, waits for them, and re-layouts, local(): key_sets[2]  3.85 us
    dot_general x1, matrix products, finish(): jnp.dot(stacked.reshape(pair_count * token_count, features), weight_block...  3.74 us
    dot_general x1, matrix products, attend(): jnp.einsum('qhd,khd->hqk', joined_q, joined_k, preferred_element_type=jnp...  3.48 us
    sub x1, other arithmetic, attend(): weights_t = (probs * (slopes - centre)).astype(jnp.bfloat16)  3.4 us
  transfers between devices with their start and end apart: 4, of which 2 were waited for; matrix products, arithmetic and copies ran while one was open for 39% of the time, Pallas kernels for 0%

commit v1 on v0

v1 whole, which is shorter than its diff:
```python
import functools
import math

import jax
import jax.numpy as jnp
from jax import lax
from jax.experimental import pallas as pl
from jax.experimental.pallas import tpu as pltpu
from jax.sharding import PartitionSpec as P

HD = 128
LOG2E = 1.4426950408889634
VMEM_LIMIT = 40 * 1024 * 1024


def swap(value, axis, mask):
    pairs = [(source, source ^ mask) for source in range(lax.axis_size(axis))]
    return lax.ppermute(value, axis, pairs)


def swap_odd(value, axis):
    pairs = []
    for low in range(1, lax.axis_size(axis) - 1, 2):
        pairs += [(low, low + 1), (low + 1, low)]
    return lax.ppermute(value, axis, pairs)


def dot_nt(a, b):
    return lax.dot_general(a, b, (((1,), (1,)), ((), ())), preferred_element_type=jnp.float32)


def score_kernel(mask, q, qt, k_own, kt_own, k_par, kt_par, k_a, k_b, p_out, w_out):
    tokens, features = q.shape
    half = k_a.shape[0] // 2
    edge = half // 2
    scaling = 1.0 / math.sqrt(HD)
    allowed = mask[...] > 0.0
    for head in range(features // HD):
        at = pl.ds(head * HD, HD)

        def ordered(own, par, at_halo):
            return jnp.concatenate(
                [
                    own[:, at],
                    par[pl.ds(0, edge), at],
                    par[pl.ds(tokens - edge, edge), at],
                    k_a[at_halo, at],
                    k_b[at_halo, at],
                    par[pl.ds(edge, tokens - 2 * edge), at],
                ],
                0,
            )

        keys = ordered(k_own, k_par, pl.ds(0, half))
        keys_t = ordered(kt_own, kt_par, pl.ds(half, half))
        query, query_t = q[:, at], qt[:, at]
        raw = jnp.where(allowed, dot_nt(query, keys), -1e30)
        top = jnp.max(raw, axis=-1, keepdims=True)
        lifted = jnp.exp2((raw - top) * (scaling * LOG2E))
        probs = lifted * (1.0 / jnp.sum(lifted, axis=-1, keepdims=True))
        slopes = scaling * dot_nt(
            jnp.concatenate([query_t, query], 1), jnp.concatenate([keys, keys_t], 1)
        )
        centre = jnp.sum(probs * slopes, axis=-1, keepdims=True)
        p_out[head] = probs.astype(jnp.bfloat16)
        w_out[head] = (probs * (slopes - centre)).astype(jnp.bfloat16)


def scores(mask, *arrays):
    tokens, features = arrays[0].shape
    heads = features // HD
    keys = mask.shape[1]
    out = jax.ShapeDtypeStruct((heads, tokens, keys), jnp.bfloat16)
    return pl.pallas_call(
        score_kernel,
        out_shape=(out, out),
        compiler_params=pltpu.CompilerParams(vmem_limit_bytes=VMEM_LIMIT),
        cost_estimate=pl.CostEstimate(
            flops=6 * heads * tokens * keys * HD, bytes_accessed=6_000_000, transcendentals=heads * tokens * keys
        ),
        name="scores",
    )(mask, *arrays)


def project_kernel(layout, step, places, gate, slope, p, w, v_own, vt_own, v_edge, v_mid, v_a, v_b, *rest):
    pieces = rest[: len(layout)]
    out_p, out_t, weight, attn, sems = rest[len(layout) :]
    tokens = v_own.shape[0]
    half = v_a.shape[0] // 2
    copies = []
    unit_at = 0
    for piece, (units, rows) in zip(pieces, layout):
        for unit in range(units):
            start = pl.multiple_of(places[unit_at] * 16, 16)
            copies.append(
                pltpu.make_async_copy(
                    piece.at[pl.ds(unit * rows, rows), :], weight.at[pl.ds(start, rows), :], sems.at[unit_at]
                )
            )
            unit_at += 1
    for copy in copies:
        copy.start()
    for head in range(p.shape[0]):
        at = pl.ds(head * HD, HD)

        def ordered(own, rows):
            return jnp.concatenate([own[:, at], v_edge[rows, at], v_a[rows, at], v_b[rows, at], v_mid[rows, at]], 0)

        values = ordered(v_own, pl.ds(0, half))
        values_t = ordered(vt_own, pl.ds(half, half))
        probs = p[head]
        primal = jnp.dot(probs, values, preferred_element_type=jnp.float32)
        tangent = jnp.dot(
            jnp.concatenate([w[head], probs], 1),
            jnp.concatenate([values, values_t], 0),
            preferred_element_type=jnp.float32,
        )
        attn[pl.ds(0, tokens), at] = primal.astype(jnp.bfloat16)
        attn[pl.ds(tokens, tokens), at] = tangent.astype(jnp.bfloat16)
    for copy in copies:
        copy.wait()
    row = pl.ds(step[0] % 8, 1)
    width = 256
    for first in range(0, weight.shape[0], width):
        cols = pl.ds(first, width)
        both = dot_nt(attn[...], weight[cols, :])
        main, main_t = both[:tokens], both[tokens:]
        gate_row, slope_row = gate[row, cols], slope[row, cols]
        out_p[:, cols] = (gate_row * main).astype(jnp.bfloat16)
        out_t[:, cols] = (gate_row * main_t + slope_row * main).astype(jnp.bfloat16)


def project(step, places, gate_table, gate_slope, probs, weights_t, values, pieces, layout):
    tokens, features = values[0].shape
    dout = gate_table.shape[1]
    units = places.shape[0]
    out = jax.ShapeDtypeStruct((tokens, dout), jnp.bfloat16)
    whole = lambda a: pl.BlockSpec(a.shape, lambda i, *_: (0,) * a.ndim)
    table = pl.BlockSpec((8, dout), lambda i, step, places: (step[0] // 8, 0))
    return pl.pallas_call(
        functools.partial(project_kernel, layout),
        out_shape=(out, out),
        grid_spec=pltpu.PrefetchScalarGridSpec(
            num_scalar_prefetch=2,
            grid=(1,),
            in_specs=[table, table, whole(probs), whole(weights_t)]
            + [whole(v) for v in values]
            + [pl.BlockSpec(memory_space=pl.ANY)] * len(pieces),
            out_specs=(whole(out), whole(out)),
            scratch_shapes=[
                pltpu.VMEM((dout, features), jnp.bfloat16),
                pltpu.VMEM((2 * tokens, features), jnp.bfloat16),
                pltpu.SemaphoreType.DMA((units,)),
            ],
        ),
        compiler_params=pltpu.CompilerParams(vmem_limit_bytes=VMEM_LIMIT),
        cost_estimate=pl.CostEstimate(
            flops=4 * tokens * features * dout, bytes_accessed=10_000_000, transcendentals=0
        ),
        name="project",
    )(step, places, gate_table, gate_slope, probs, weights_t, *values, *pieces)


def gather_weight(block):
    columns = block.shape[0]
    tm, height, fsdp = (lax.axis_size(axis) for axis in ("tm", "height", "fsdp"))
    rows = columns // 4
    if (tm % 4, height, fsdp) != (0, 2, 4) or rows % 16 != 0:
        full = lax.all_gather(block, ("height", "fsdp"), axis=0, tiled=True)
        return [full], [(1, full.shape[0])], jnp.zeros((1,), jnp.int32)
    mine = lax.axis_index("tm") % 4
    h, f = lax.axis_index("height"), lax.axis_index("fsdp")
    quarter = lax.dynamic_slice_in_dim(block, mine * rows, rows, 0)
    other = swap(quarter, "height", 1)
    own3 = swap(quarter, "fsdp", 3)
    own2 = swap(quarter, "fsdp", 2)
    both1 = swap(jnp.concatenate([quarter, other], 0), "fsdp", 1)
    other3 = swap(other, "fsdp", 3)
    other2 = swap(other, "fsdp", 2)
    held_a = jnp.concatenate([other, own3], 0)
    cross_a = swap(held_a, "tm", 2)
    held_b = jnp.concatenate([both1, own2], 0)
    cross_b = swap(held_b, "tm", 2)
    held_c = jnp.concatenate([other3, other2], 0)
    cross_c = swap(held_c, "tm", 2)
    first = jnp.concatenate([held_a, held_b, cross_a, cross_b], 0)
    second = jnp.concatenate([held_c, cross_c], 0)
    near_first = swap(first, "tm", 1)
    near_second = swap(second, "tm", 1)
    in_a, in_b, in_c = [(1, 0), (0, 3)], [(0, 1), (1, 1), (0, 2)], [(1, 3), (1, 2)]

    def place(kinds, mask):
        return [((((h ^ dh) * fsdp + (f ^ df)) * 4 + (mine ^ mask)) * rows) // 16 for dh, df in kinds]

    spots = [((h * fsdp + f) * columns) // 16]
    for mask in (0, 1):
        spots += place(in_a + in_b, mask) + place(in_a + in_b, mask ^ 2)
    for mask in (0, 1):
        spots += place(in_c, mask) + place(in_c, mask ^ 2)
    pieces = [block, first, near_first, second, near_second]
    layout = [(1, columns), (10, rows), (10, rows), (4, rows), (4, rows)]
    return pieces, layout, jnp.stack(spots).astype(jnp.int32)


def local(
    query_primal,
    key_primal,
    value_primal,
    query_tangent,
    key_tangent,
    value_tangent,
    out_weight,
    gate_table,
    gate_slope,
    timestep,
):
    _, frames, rows, columns, features = query_primal.shape
    per_frame = rows * columns
    tokens = frames * per_frame
    flat = lambda x: x.reshape(tokens, features)
    q, qt, k, kt, v, vt = map(
        flat, (query_primal, query_tangent, key_primal, key_tangent, value_primal, value_tangent)
    )
    last = tokens - per_frame
    pieces, layout, places = gather_weight(out_weight.T)
    k_par = swap(k, "height", 1)
    kt_par = swap(kt, "height", 1)
    v_edge = swap(
        jnp.concatenate([v[:per_frame], v[last:], vt[:per_frame], vt[last:]], 0), "height", 1
    )
    v_mid = swap(jnp.concatenate([v[per_frame:last], vt[per_frame:last]], 0), "height", 1)
    tm = lax.axis_index("tm")
    even = tm % 2 == 0

    def end(array, from_last):
        start = jnp.where(from_last, array.shape[0] - per_frame, 0)
        return lax.dynamic_slice_in_dim(array, start, per_frame, 0)

    def halo(own, par, own_t, par_t):
        to_a = jnp.concatenate([end(a, even) for a in (own, par, own_t, par_t)], 0)
        to_b = jnp.concatenate([end(a, ~even) for a in (own, par, own_t, par_t)], 0)
        return swap(to_a, "tm", 1), swap_odd(to_b, "tm")

    k_a, k_b = halo(k, k_par, kt, kt_par)
    v_a, v_b = halo(v, v_edge[: 2 * per_frame], vt, v_edge[2 * per_frame :])
    inside = (tm > 0) & (tm < lax.axis_size("tm") - 1)
    spot = lax.broadcasted_iota(jnp.int32, (1, 2 * tokens + 4 * per_frame), 1)
    b_start = tokens + 4 * per_frame
    is_b = (spot >= b_start) & (spot < b_start + 2 * per_frame)
    mask = jnp.where(is_b & ~inside, 0.0, 1.0)
    probs, weights_t = scores(mask, q, qt, k, kt, k_par, kt_par, k_a, k_b)
    out_p, out_t = project(
        timestep, places, gate_table, gate_slope, probs, weights_t, (v, vt, v_edge, v_mid, v_a, v_b), pieces, layout
    )
    shape = query_primal.shape[:-1] + (out_p.shape[1],)
    return out_p.reshape(shape), out_t.reshape(shape)


def solution(mesh):
    token_spec = P("fsdp", "tm", "height", None, None)
    in_specs = (token_spec,) * 6 + (P(None, ("height", "fsdp")), P(), P(), P("fsdp"))
    return jax.shard_map(
        local, mesh=mesh, in_specs=in_specs, out_specs=(token_spec, token_spec), check_vma=False
    )
```

time: 118 us -> 93.2 us (0.79)
  the two profiles are of different devices: /device:TPU:1 before, /device:TPU:9 now
where the time goes in v1:
time: 93.2 us; the launch traced here: 92.6 us
  waiting for transfers between devices  32.6 us (35%)
  starting transfers between devices  29.3 us (31%)
  local copies, waits for them, and re-layouts  12.8 us (14%)
  Pallas kernels  12.5 us (13%)
  between operations  2.75 us (3%)
  other arithmetic  2.56 us (3%)
    ppermute x17, waiting for transfers between devices, swap(): return lax.ppermute(value, axis, pairs)  32.6 us
    ppermute x2, starting transfers between devices, swap_odd(): return lax.ppermute(value, axis, pairs)  14.8 us
    ppermute x17, starting transfers between devices, swap(): return lax.ppermute(value, axis, pairs)  14.5 us
    pallas_call x1, Pallas kernels, project(): pl.pallas_call(functools.partial(project_kernel, layout), out_shape=(out,...  9.43 us
    unnamed x37, local copies, waits for them, and re-layouts  7.6 us
    pallas_call x1, Pallas kernels, scores(): pl.pallas_call(score_kernel, out_shape=(out, out), compiler_params=pltpu....  3.11 us
    dynamic_slice x6, local copies, waits for them, and re-layouts, end(): return lax.dynamic_slice_in_dim(array, start, per_frame, 0)  2.02 us
  transfers between devices with their start and end apart: 19, of which 5 were waited for; matrix products, arithmetic and copies ran while one was open for 7% of the time, Pallas kernels for 3%

profile of v1, /device:TPU:9, one launch (start us, length us, event | category | flops | bytes accessed | tf_op | source)
XLA Modules:
  0.0 92.6 jit_solution(5614970407039979353)
XLA Ops:
  0.7 1.0 %dynamic-slice_bitcast_fusion = bf16[48,1536]{1,0:T(8,128)(2,1)S(1)} fusion(bf16[1536,192]{0,1:T(8,128)(2,1)} %param.16, s32[]{:T(128)S(6)} %select_n.183), kind=kLoop, calls=%fused_computation.10 | loop fusion | bytes 294916 | tf_op jit(solution)/shard_map/dynamic_slice | solution.py:173
  1.7 1.3 %collective-permute-start.8 = (bf16[48,1536]{1,0:T(8,128)(2,1)S(1)}, bf16[48,1536]{1,0:T(8,128)(2,1)S(1)}, u32[]{:S(2)}, u32[]{:S(2)}) collective-permute-start(bf16[48,1536]{1,0:T(8,128)(2,1)S(1)} %dynamic-slice_bitcast_fusion), channel_id=1, source_target_pairs={{0,4},{4,0},{1,5},{5,1},{2,6},{6,2},{3,7},{7,3},{8,12},{12,8},{9,1... | collective-permute-start | bytes 442376 | tf_op jit(solution)/shard_map/ppermute | solution.py:18
  3.0 1.3 %collective-permute-start.9 = (bf16[48,1536]{1,0:T(8,128)(2,1)S(1)}, bf16[48,1536]{1,0:T(8,128)(2,1)S(1)}, u32[]{:S(2)}, u32[]{:S(2)}) collective-permute-start(bf16[48,1536]{1,0:T(8,128)(2,1)S(1)} %dynamic-slice_bitcast_fusion), channel_id=1, source_target_pairs={{0,3},{1,2},{2,1},{3,0},{4,7},{5,6},{6,5},{7,4},{8,11},{9,10},{10,... | collective-permute-start | bytes 442376 | tf_op jit(solution)/shard_map/ppermute | solution.py:18
  4.3 1.0 %collective-permute-start.11 = (bf16[48,1536]{1,0:T(8,128)(2,1)S(1)}, bf16[48,1536]{1,0:T(8,128)(2,1)S(1)}, u32[]{:S(2)}, u32[]{:S(2)}) collective-permute-start(bf16[48,1536]{1,0:T(8,128)(2,1)S(1)} %dynamic-slice_bitcast_fusion), channel_id=1, source_target_pairs={{0,2},{1,3},{2,0},{3,1},{4,6},{5,7},{6,4},{7,5},{8,10},{9,11},{10,... | collective-permute-start | bytes 442376 | tf_op jit(solution)/shard_map/ppermute | solution.py:18
  5.6 1.2 %collective-permute-start.1 = (bf16[128,1536]{1,0:T(8,128)(2,1)}, bf16[128,1536]{1,0:T(8,128)(2,1)}, u32[]{:S(2)}, u32[]{:S(2)}) collective-permute-start(bf16[128,1536]{1,0:T(8,128)(2,1)} %bitcast.58), channel_id=1, source_target_pairs={{0,4},{4,0},{1,5},{5,1},{2,6},{6,2},{3,7},{7,3},{8,12},{12,8},{9,1... | collective-permute-start | bytes 1179656 | tf_op jit(solution)/shard_map/ppermute | solution.py:18
  7.8 1.1 %slice_bitcast_fusion.1 = (bf16[32,1536]{1,0:T(8,128)(2,1)S(1)}, bf16[32,1536]{1,0:T(8,128)(2,1)S(1)}, bf16[32,1536]{1,0:T(8,128)(2,1)S(1)}, bf16[32,1536]{1,0:T(8,128)(2,1)S(1)}) fusion(bf16[1,4,4,8,1536]{4,3,2,1,0:T(8,128)(2,1)} %param.15, bf16[1,4,4,8,1536]{4,3,2,1,0:T(8,128)(2,1)} %param.12), kind=kLoop, calls=%fused_computation.12 | loop fusion | bytes 786432 | tf_op jit(solution)/shard_map/slice | solution.py:229
  9.8 2.4 %collective-permute-start.15 = (bf16[48,1536]{1,0:T(8,128)(2,1)S(1)}, bf16[48,1536]{1,0:T(8,128)(2,1)S(1)}, u32[]{:S(2)}, u32[]{:S(2)}) collective-permute-start(bf16[48,1536]{1,0:T(8,128)(2,1)S(1)} %collective-permute-done.8), channel_id=1, source_target_pairs={{0,3},{1,2},{2,1},{3,0},{4,7},{5,6},{6,5},{7,4},{8,11},{9,10},{10,... | collective-permute-start | bytes 442376 | tf_op jit(solution)/shard_map/ppermute | solution.py:18
  12.2 2.1 %collective-permute-done.9 = bf16[48,1536]{1,0:T(8,128)(2,1)S(1)} collective-permute-done((bf16[48,1536]{1,0:T(8,128)(2,1)S(1)}, bf16[48,1536]{1,0:T(8,128)(2,1)S(1)}, u32[]{:S(2)}, u32[]{:S(2)}) %collective-permute-start.9) | collective-permute-done | bytes 147488 | tf_op jit(solution)/shard_map/ppermute | solution.py:18
  14.4 10.9 %collective-permute-done.15 = bf16[48,1536]{1,0:T(8,128)(2,1)S(1)} collective-permute-done((bf16[48,1536]{1,0:T(8,128)(2,1)S(1)}, bf16[48,1536]{1,0:T(8,128)(2,1)S(1)}, u32[]{:S(2)}, u32[]{:S(2)}) %collective-permute-start.15) | collective-permute-done | bytes 147488 | tf_op jit(solution)/shard_map/ppermute | solution.py:18
  25.6 3.0 %collective-permute-done.16 = bf16[48,1536]{1,0:T(8,128)(2,1)S(1)} collective-permute-done((bf16[48,1536]{1,0:T(8,128)(2,1)S(1)}, bf16[48,1536]{1,0:T(8,128)(2,1)S(1)}, u32[]{:S(2)}, u32[]{:S(2)}) %collective-permute-start.16) | collective-permute-done | bytes 147488 | tf_op jit(solution)/shard_map/ppermute | solution.py:18
  29.0 2.6 %collective-permute-start.10 = (bf16[96,1536]{1,0:T(8,128)(2,1)S(1)}, bf16[96,1536]{1,0:T(8,128)(2,1)S(1)}, u32[]{:S(2)}, u32[]{:S(2)}) collective-permute-start(bf16[96,1536]{1,0:T(8,128)(2,1)S(1)} %get-tuple-element.33), channel_id=1, source_target_pairs={{0,1},{1,0},{2,3},{3,2},{4,5},{5,4},{6,7},{7,6},{8,9},{9,8},{10,11... | collective-permute-start | bytes 884744 | tf_op jit(solution)/shard_map/ppermute | solution.py:18
  32.5 1.3 %collective-permute-start.12 = (bf16[96,1536]{1,0:T(8,128)(2,1)S(1)}, bf16[96,1536]{1,0:T(8,128)(2,1)S(1)}, u32[]{:S(2)}, u32[]{:S(2)}) collective-permute-start(bf16[96,1536]{1,0:T(8,128)(2,1)S(1)} %get-tuple-element.32), channel_id=1, source_target_pairs={{0,16},{8,24},{16,0},{24,8},{1,17},{9,25},{17,1},{25,9},{2,18},{10... | collective-permute-start | bytes 884744 | tf_op jit(solution)/shard_map/ppermute | solution.py:18
  35.2 12.0 %collective-permute-start.3 = (bf16[128,1536]{1,0:T(8,128)(2,1)S(1)}, bf16[128,1536]{1,0:T(8,128)(2,1)S(1)}, u32[]{:S(2)}, u32[]{:S(2)}) collective-permute-start(bf16[128,1536]{1,0:T(8,128)(2,1)S(1)} %pad_maximum_fusion.2), channel_id=1, source_target_pairs={{8,16},{16,8},{9,17},{17,9},{10,18},{18,10},{11,19},{19,11},{12,20... | collective-permute-start | bytes 1179656 | tf_op jit(solution)/shard_map/ppermute | solution.py:25
  47.4 15.8 %collective-permute-done.13 = bf16[144,1536]{1,0:T(8,128)(2,1)S(1)} collective-permute-done((bf16[144,1536]{1,0:T(8,128)(2,1)S(1)}, bf16[144,1536]{1,0:T(8,128)(2,1)S(1)}, u32[]{:S(2)}, u32[]{:S(2)}) %collective-permute-start.13) | collective-permute-done | bytes 442400 | tf_op jit(solution)/shard_map/ppermute | solution.py:18
  63.3 1.4 %collective-permute-start.14 = (bf16[480,1536]{1,0:T(8,128)(2,1)S(1)}, bf16[480,1536]{1,0:T(8,128)(2,1)}, u32[]{:S(2)}, u32[]{:S(2)}) collective-permute-start(bf16[480,1536]{1,0:T(8,128)(2,1)S(1)} %constant_dynamic-update-slice_fusion.rest_1_), channel_id=1, source_target_pairs={{0,8},{8,0},{16,24},{24,16},{1,9},{9,1},{17,25},{25,17},{2,10},{10... | collective-permute-start | bytes 4423688 | tf_op jit(solution)/shard_map/ppermute | solution.py:18
  69.3 2.8 %collective-permute-start.7 = (bf16[128,1536]{1,0:T(8,128)(2,1)}, bf16[128,1536]{1,0:T(8,128)(2,1)}, u32[]{:S(2)}, u32[]{:S(2)}) collective-permute-start(bf16[128,1536]{1,0:T(8,128)(2,1)} %pad_maximum_fusion.6), channel_id=1, source_target_pairs={{8,16},{16,8},{9,17},{17,9},{10,18},{18,10},{11,19},{19,11},{12,20... | collective-permute-start | bytes 1179656 | tf_op jit(solution)/shard_map/ppermute | solution.py:25
  74.0 1.0 %copy-done.4 = bf16[1,4,4,8,1536]{4,3,2,1,0:T(8,128)(2,1)S(1)} copy-done((bf16[1,4,4,8,1536]{4,3,2,1,0:T(8,128)(2,1)S(1)}, bf16[1,4,4,8,1536]{4,3,2,1,0:T(8,128)(2,1)}, u32[]{:S(2)}) %copy-start.4) | copy-done | bytes 393240
  75.0 1.0 %copy-done.6 = bf16[1,4,4,8,1536]{4,3,2,1,0:T(8,128)(2,1)S(1)} copy-done((bf16[1,4,4,8,1536]{4,3,2,1,0:T(8,128)(2,1)S(1)}, bf16[1,4,4,8,1536]{4,3,2,1,0:T(8,128)(2,1)}, u32[]{:S(2)}) %copy-start.6) | copy-done | bytes 393240
  76.0 1.0 %copy-done.7 = bf16[1,4,4,8,1536]{4,3,2,1,0:T(8,128)(2,1)S(1)} copy-done((bf16[1,4,4,8,1536]{4,3,2,1,0:T(8,128)(2,1)S(1)}, bf16[1,4,4,8,1536]{4,3,2,1,0:T(8,128)(2,1)}, u32[]{:S(2)}) %copy-start.7) | copy-done | bytes 393240
  77.0 1.0 %copy-done.8 = bf16[1,4,4,8,1536]{4,3,2,1,0:T(8,128)(2,1)S(1)} copy-done((bf16[1,4,4,8,1536]{4,3,2,1,0:T(8,128)(2,1)S(1)}, bf16[1,4,4,8,1536]{4,3,2,1,0:T(8,128)(2,1)}, u32[]{:S(2)}) %copy-start.8) | copy-done | bytes 393240
  78.0 1.0 %copy-done.10 = bf16[128,1536]{1,0:T(8,128)(2,1)S(1)} copy-done((bf16[128,1536]{1,0:T(8,128)(2,1)S(1)}, bf16[128,1536]{1,0:T(8,128)(2,1)}, u32[]{:S(2)}) %copy-start.10) | copy-done | bytes 393240
  79.0 1.0 %copy-done.12 = bf16[128,1536]{1,0:T(8,128)(2,1)S(1)} copy-done((bf16[128,1536]{1,0:T(8,128)(2,1)S(1)}, bf16[128,1536]{1,0:T(8,128)(2,1)}, u32[]{:S(2)}) %copy-start.12) | copy-done | bytes 393240
  80.0 3.1 %scores.1 = (bf16[12,128,384]{2,1,0:T(8,128)(2,1)S(1)}, bf16[12,128,384]{2,1,0:T(8,128)(2,1)S(1)}) custom-call(f32[1,384]{1,0:T(1,128)S(1)} %and_select_fusion.mask, bf16[128,1536]{1,0:T(8,128)(2,1)S(1)} %bitcast.61, bf16[128,1536]{1,0:T(8,128)(2,1)S(1)} %bitcast.62, bf16[128,1536]{1,0:T(8,128)(2,1)S(1)} %bitcast.57, bf16[128,1536]{1,0:T(8,128)(2,1)S(1)} %bitcast.60, ...), custom_call_target="tpu_custom_call" | custom-call | flops 452984832 | bytes 6000000 | tf_op jit(solution)/shard_map/scores/pallas_call | solution.py:74
  83.2 9.4 %project.1 = (bf16[128,1536]{1,0:T(8,128)(2,1)}, bf16[128,1536]{1,0:T(8,128)(2,1)}) custom-call(s32[1]{0:T(128)S(6)} %copy.19.step, s32[29]{0:T(128)S(1)} %stack.119.places, f32[64,1536]{1,0:T(8,128)S(1)} %copy-done.13, f32[64,1536]{1,0:T(8,128)S(1)} %copy-done.14, bf16[12,128,384]{2,1,0:T(8,128)(2,1)S(1)} %get-tuple-element.6.p, ...), custom_call_target="tpu_custom_call" | custom-call | flops 1207959552 | bytes 10000000 | tf_op jit(solution)/shard_map/project/pallas_call | solution.py:140
  (77 shorter events, 10.0 us)
Async XLA Ops:
  0.6 8.2 %copy-start.3 = (bf16[1,4,4,8,1536]{4,3,2,1,0:T(8,128)(2,1)S(1)}, bf16[1,4,4,8,1536]{4,3,2,1,0:T(8,128)(2,1)}, u32[]{:S(2)}) copy-start(bf16[1,4,4,8,1536]{4,3,2,1,0:T(8,128)(2,1)} %param.11) | copy-start | bytes 1179652
  0.6 8.3 %copy-start = (bf16[1,4,4,8,1536]{4,3,2,1,0:T(8,128)(2,1)S(1)}, bf16[1,4,4,8,1536]{4,3,2,1,0:T(8,128)(2,1)}, u32[]{:S(2)}) copy-start(bf16[1,4,4,8,1536]{4,3,2,1,0:T(8,128)(2,1)} %param.12) | copy-start | bytes 1179652
  0.7 8.2 %copy-start.1 = (bf16[1,4,4,8,1536]{4,3,2,1,0:T(8,128)(2,1)S(1)}, bf16[1,4,4,8,1536]{4,3,2,1,0:T(8,128)(2,1)}, u32[]{:S(2)}) copy-start(bf16[1,4,4,8,1536]{4,3,2,1,0:T(8,128)(2,1)} %param.15) | copy-start | bytes 1179652
  0.7 8.2 %copy-start.5 = (bf16[1,4,4,8,1536]{4,3,2,1,0:T(8,128)(2,1)S(1)}, bf16[1,4,4,8,1536]{4,3,2,1,0:T(8,128)(2,1)}, u32[]{:S(2)}) copy-start(bf16[1,4,4,8,1536]{4,3,2,1,0:T(8,128)(2,1)} %param.14) | copy-start | bytes 1179652
  1.7 8.1 %collective-permute-start.8 = (bf16[48,1536]{1,0:T(8,128)(2,1)S(1)}, bf16[48,1536]{1,0:T(8,128)(2,1)S(1)}, u32[]{:S(2)}, u32[]{:S(2)}) collective-permute-start(bf16[48,1536]{1,0:T(8,128)(2,1)S(1)} %dynamic-slice_bitcast_fusion), channel_id=1, source_target_pairs={{0,4},{4,0},{1,5},{5,1},{2,6},{6,2},{3,7},{7,3},{8,12},{12,8},{9,1... | collective-permute-start | bytes 442376 | tf_op jit(solution)/shard_map/ppermute | solution.py:18
  3.0 11.3 %collective-permute-start.9 = (bf16[48,1536]{1,0:T(8,128)(2,1)S(1)}, bf16[48,1536]{1,0:T(8,128)(2,1)S(1)}, u32[]{:S(2)}, u32[]{:S(2)}) collective-permute-start(bf16[48,1536]{1,0:T(8,128)(2,1)S(1)} %dynamic-slice_bitcast_fusion), channel_id=1, source_target_pairs={{0,3},{1,2},{2,1},{3,0},{4,7},{5,6},{6,5},{7,4},{8,11},{9,10},{10,... | collective-permute-start | bytes 442376 | tf_op jit(solution)/shard_map/ppermute | solution.py:18
  4.3 30.9 %collective-permute-start.11 = (bf16[48,1536]{1,0:T(8,128)(2,1)S(1)}, bf16[48,1536]{1,0:T(8,128)(2,1)S(1)}, u32[]{:S(2)}, u32[]{:S(2)}) collective-permute-start(bf16[48,1536]{1,0:T(8,128)(2,1)S(1)} %dynamic-slice_bitcast_fusion), channel_id=1, source_target_pairs={{0,2},{1,3},{2,0},{3,1},{4,6},{5,7},{6,4},{7,5},{8,10},{9,11},{10,... | collective-permute-start | bytes 442376 | tf_op jit(solution)/shard_map/ppermute | solution.py:18
  5.3 23.6 %collective-permute-start = (bf16[128,1536]{1,0:T(8,128)(2,1)}, bf16[128,1536]{1,0:T(8,128)(2,1)}, u32[]{:S(2)}, u32[]{:S(2)}) collective-permute-start(bf16[128,1536]{1,0:T(8,128)(2,1)} %bitcast.55), channel_id=1, source_target_pairs={{0,4},{4,0},{1,5},{5,1},{2,6},{6,2},{3,7},{7,3},{8,12},{12,8},{9,1... | collective-permute-start | bytes 1179656 | tf_op jit(solution)/shard_map/ppermute | solution.py:18
  5.6 28.3 %collective-permute-start.1 = (bf16[128,1536]{1,0:T(8,128)(2,1)}, bf16[128,1536]{1,0:T(8,128)(2,1)}, u32[]{:S(2)}, u32[]{:S(2)}) collective-permute-start(bf16[128,1536]{1,0:T(8,128)(2,1)} %bitcast.58), channel_id=1, source_target_pairs={{0,4},{4,0},{1,5},{5,1},{2,6},{6,2},{3,7},{7,3},{8,12},{12,8},{9,1... | collective-permute-start | bytes 1179656 | tf_op jit(solution)/shard_map/ppermute | solution.py:18
  9.8 15.5 %collective-permute-start.15 = (bf16[48,1536]{1,0:T(8,128)(2,1)S(1)}, bf16[48,1536]{1,0:T(8,128)(2,1)S(1)}, u32[]{:S(2)}, u32[]{:S(2)}) collective-permute-start(bf16[48,1536]{1,0:T(8,128)(2,1)S(1)} %collective-permute-done.8), channel_id=1, source_target_pairs={{0,3},{1,2},{2,1},{3,0},{4,7},{5,6},{6,5},{7,4},{8,11},{9,10},{10,... | collective-permute-start | bytes 442376 | tf_op jit(solution)/shard_map/ppermute | solution.py:18
  14.3 14.3 %collective-permute-start.16 = (bf16[48,1536]{1,0:T(8,128)(2,1)S(1)}, bf16[48,1536]{1,0:T(8,128)(2,1)S(1)}, u32[]{:S(2)}, u32[]{:S(2)}) collective-permute-start(bf16[48,1536]{1,0:T(8,128)(2,1)S(1)} %collective-permute-done.8), channel_id=1, source_target_pairs={{0,2},{1,3},{2,0},{3,1},{4,6},{5,7},{6,4},{7,5},{8,10},{9,11},{10,... | collective-permute-start | bytes 442376 | tf_op jit(solution)/shard_map/ppermute | solution.py:18
  25.3 7.2 %collective-permute-start.4 = (bf16[128,1536]{1,0:T(8,128)(2,1)S(1)}, bf16[128,1536]{1,0:T(8,128)(2,1)S(1)}, u32[]{:S(2)}, u32[]{:S(2)}) collective-permute-start(bf16[128,1536]{1,0:T(8,128)(2,1)S(1)} %pad_maximum_fusion.3), channel_id=1, source_target_pairs={{0,4},{4,0},{1,5},{5,1},{2,6},{6,2},{3,7},{7,3},{8,12},{12,8},{9,1... | collective-permute-start | bytes 1179656 | tf_op jit(solution)/shard_map/ppermute | solution.py:18
  28.7 54.4 %collective-permute-start.5 = (bf16[128,1536]{1,0:T(8,128)(2,1)}, bf16[128,1536]{1,0:T(8,128)(2,1)}, u32[]{:S(2)}, u32[]{:S(2)}) collective-permute-start(bf16[128,1536]{1,0:T(8,128)(2,1)} %pad_maximum_fusion.4), channel_id=1, source_target_pairs={{0,4},{4,0},{1,5},{5,1},{2,6},{6,2},{3,7},{7,3},{8,12},{12,8},{9,1... | collective-permute-start | bytes 1179656 | tf_op jit(solution)/shard_map/ppermute | solution.py:18
  29.0 18.3 %collective-permute-start.10 = (bf16[96,1536]{1,0:T(8,128)(2,1)S(1)}, bf16[96,1536]{1,0:T(8,128)(2,1)S(1)}, u32[]{:S(2)}, u32[]{:S(2)}) collective-permute-start(bf16[96,1536]{1,0:T(8,128)(2,1)S(1)} %get-tuple-element.33), channel_id=1, source_target_pairs={{0,1},{1,0},{2,3},{3,2},{4,5},{5,4},{6,7},{7,6},{8,9},{9,8},{10,11... | collective-permute-start | bytes 884744 | tf_op jit(solution)/shard_map/ppermute | solution.py:18
  32.5 14.8 %collective-permute-start.12 = (bf16[96,1536]{1,0:T(8,128)(2,1)S(1)}, bf16[96,1536]{1,0:T(8,128)(2,1)S(1)}, u32[]{:S(2)}, u32[]{:S(2)}) collective-permute-start(bf16[96,1536]{1,0:T(8,128)(2,1)S(1)} %get-tuple-element.32), channel_id=1, source_target_pairs={{0,16},{8,24},{16,0},{24,8},{1,17},{9,25},{17,1},{25,9},{2,18},{10... | collective-permute-start | bytes 884744 | tf_op jit(solution)/shard_map/ppermute | solution.py:18
  33.9 31.8 %collective-permute-start.17 = (bf16[96,1536]{1,0:T(8,128)(2,1)S(1)}, bf16[96,1536]{1,0:T(8,128)(2,1)S(1)}, u32[]{:S(2)}, u32[]{:S(2)}) collective-permute-start(bf16[96,1536]{1,0:T(8,128)(2,1)S(1)} %pad_maximum_fusion.9), channel_id=1, source_target_pairs={{0,16},{8,24},{16,0},{24,8},{1,17},{9,25},{17,1},{25,9},{2,18},{10... | collective-permute-start | bytes 884744 | tf_op jit(solution)/shard_map/ppermute | solution.py:18
  35.2 31.8 %collective-permute-start.3 = (bf16[128,1536]{1,0:T(8,128)(2,1)S(1)}, bf16[128,1536]{1,0:T(8,128)(2,1)S(1)}, u32[]{:S(2)}, u32[]{:S(2)}) collective-permute-start(bf16[128,1536]{1,0:T(8,128)(2,1)S(1)} %pad_maximum_fusion.2), channel_id=1, source_target_pairs={{8,16},{16,8},{9,17},{17,9},{10,18},{18,10},{11,19},{19,11},{12,20... | collective-permute-start | bytes 1179656 | tf_op jit(solution)/shard_map/ppermute | solution.py:25
  47.3 16.0 %collective-permute-start.13 = (bf16[144,1536]{1,0:T(8,128)(2,1)S(1)}, bf16[144,1536]{1,0:T(8,128)(2,1)S(1)}, u32[]{:S(2)}, u32[]{:S(2)}) collective-permute-start(bf16[144,1536]{1,0:T(8,128)(2,1)S(1)} %pad_maximum_fusion), channel_id=1, source_target_pairs={{0,16},{8,24},{16,0},{24,8},{1,17},{9,25},{17,1},{25,9},{2,18},{10... | collective-permute-start | bytes 1327112 | tf_op jit(solution)/shard_map/ppermute | solution.py:18
  63.3 19.9 %collective-permute-start.14 = (bf16[480,1536]{1,0:T(8,128)(2,1)S(1)}, bf16[480,1536]{1,0:T(8,128)(2,1)}, u32[]{:S(2)}, u32[]{:S(2)}) collective-permute-start(bf16[480,1536]{1,0:T(8,128)(2,1)S(1)} %constant_dynamic-update-slice_fusion.rest_1_), channel_id=1, source_target_pairs={{0,8},{8,0},{16,24},{24,16},{1,9},{9,1},{17,25},{25,17},{2,10},{10... | collective-permute-start | bytes 4423688 | tf_op jit(solution)/shard_map/ppermute | solution.py:18
  64.8 3.8 %collective-permute-start.2 = (bf16[128,1536]{1,0:T(8,128)(2,1)S(1)}, bf16[128,1536]{1,0:T(8,128)(2,1)S(1)}, u32[]{:S(2)}, u32[]{:S(2)}) collective-permute-start(bf16[128,1536]{1,0:T(8,128)(2,1)S(1)} %pad_maximum_fusion.1), channel_id=1, source_target_pairs={{0,8},{8,0},{16,24},{24,16},{1,9},{9,1},{17,25},{25,17},{2,10},{10... | collective-permute-start | bytes 1179656 | tf_op jit(solution)/shard_map/ppermute | solution.py:18
  65.7 17.5 %collective-permute-start.18 = (bf16[192,1536]{1,0:T(8,128)(2,1)S(1)}, bf16[192,1536]{1,0:T(8,128)(2,1)}, u32[]{:S(2)}, u32[]{:S(2)}) collective-permute-start(bf16[192,1536]{1,0:T(8,128)(2,1)S(1)} %constant_dynamic-update-slice_fusion.6.rest_3_), channel_id=1, source_target_pairs={{0,8},{8,0},{16,24},{24,16},{1,9},{9,1},{17,25},{25,17},{2,10},{10... | collective-permute-start | bytes 1769480 | tf_op jit(solution)/shard_map/ppermute | solution.py:18
  67.8 15.3 %collective-permute-start.6 = (bf16[128,1536]{1,0:T(8,128)(2,1)}, bf16[128,1536]{1,0:T(8,128)(2,1)}, u32[]{:S(2)}, u32[]{:S(2)}) collective-permute-start(bf16[128,1536]{1,0:T(8,128)(2,1)} %pad_maximum_fusion.5), channel_id=1, source_target_pairs={{0,8},{8,0},{16,24},{24,16},{1,9},{9,1},{17,25},{25,17},{2,10},{10... | collective-permute-start | bytes 1179656 | tf_op jit(solution)/shard_map/ppermute | solution.py:18
  69.3 13.8 %collective-permute-start.7 = (bf16[128,1536]{1,0:T(8,128)(2,1)}, bf16[128,1536]{1,0:T(8,128)(2,1)}, u32[]{:S(2)}, u32[]{:S(2)}) collective-permute-start(bf16[128,1536]{1,0:T(8,128)(2,1)} %pad_maximum_fusion.6), channel_id=1, source_target_pairs={{8,16},{16,8},{9,17},{17,9},{10,18},{18,10},{11,19},{19,11},{12,20... | collective-permute-start | bytes 1179656 | tf_op jit(solution)/shard_map/ppermute | solution.py:25
  80.0 3.2 %copy-start.14 = (f32[64,1536]{1,0:T(8,128)S(1)}, f32[64,1536]{1,0:T(8,128)}, u32[]{:S(2)}) copy-start(f32[64,1536]{1,0:T(8,128)} %slope.1) | copy-start | bytes 1179652
  (10 other events, 13.8 us)

commit v2 on v1

v2 whole, which is shorter than its diff:
```python
import math

import jax
import jax.numpy as jnp
from jax import lax
from jax.experimental import pallas as pl
from jax.experimental.pallas import tpu as pltpu
from jax.sharding import PartitionSpec as P

HD = 128
ORDER = {
    "k_par": ["own"],
    "twos": ["own_parts"],
    "half": ["own_parts"],
    "threes": ["k_par"],
    "cross": ["near_b"],
    "v_mid": ["threes"],
    "near": ["v_mid"],
    "gates": ["twos"],
    "late_parts": ["threes"],
}
LOG2E = 1.4426950408889634
VMEM_LIMIT = 24 * 1024 * 1024
SMALL = pl.CostEstimate(flops=1, bytes_accessed=1, transcendentals=0)
SCORES_COST = pl.CostEstimate(flops=20_000_000_000, bytes_accessed=1, transcendentals=0)


def swap(value, axis, mask):
    pairs = [(source, source ^ mask) for source in range(lax.axis_size(axis))]
    return lax.ppermute(value, axis, pairs)


def swap_odd(value, axis):
    pairs = []
    for low in range(1, lax.axis_size(axis) - 1, 2):
        pairs += [(low, low + 1), (low + 1, low)]
    return lax.ppermute(value, axis, pairs)


def dot_nt(a, b):
    return lax.dot_general(a, b, (((1,), (1,)), ((), ())), preferred_element_type=jnp.float32)


def after(value, *done):
    return lax.optimization_barrier((value,) + done)[0]


def gather_rows(name, outs, moves, sources, limit=VMEM_LIMIT):
    features = sources[0].shape[1]

    def kernel(*refs):
        even = lax.axis_index("tm") & 1 == 0
        ins, rest, sems = refs[: len(sources)], refs[len(sources) : -1], refs[-1]
        copies = []
        for i, (source, row, out, to, count) in enumerate(moves):
            if isinstance(row, tuple):
                row = pl.multiple_of(jnp.where(even, *row), 16)
            copies.append(
                pltpu.make_async_copy(
                    ins[source].at[pl.ds(row, count), :], rest[out].at[pl.ds(to, count), :], sems.at[i]
                )
            )
        for copy in copies:
            copy.start()
        for copy in copies:
            copy.wait()

    return pl.pallas_call(
        kernel,
        out_shape=[jax.ShapeDtypeStruct((n, features), sources[0].dtype) for n in outs],
        in_specs=[pl.BlockSpec(memory_space=pl.ANY)] * len(sources),
        out_specs=[pl.BlockSpec(memory_space=pltpu.VMEM)] * len(outs),
        scratch_shapes=[pltpu.SemaphoreType.DMA((len(moves),))],
        compiler_params=pltpu.CompilerParams(vmem_limit_bytes=limit),
        cost_estimate=SMALL,
        name=name,
    )(*sources)


def table_rows(step, gate_table, gate_slope):
    features = gate_table.shape[1]

    def kernel(step, gate, slope, gate_row, slope_row):
        row = pl.ds(step[0] & 7, 1)
        gate_row[...] = gate[row, :]
        slope_row[...] = slope[row, :]

    table = pl.BlockSpec((8, features), lambda i, step: (step[0] >> 3, 0))
    one = pl.BlockSpec((1, features), lambda i, step: (0, 0))
    return pl.pallas_call(
        kernel,
        out_shape=[jax.ShapeDtypeStruct((1, features), gate_table.dtype)] * 2,
        grid_spec=pltpu.PrefetchScalarGridSpec(
            num_scalar_prefetch=1, grid=(1,), in_specs=[table, table], out_specs=[one, one]
        ),
        compiler_params=pltpu.CompilerParams(vmem_limit_bytes=VMEM_LIMIT),
        cost_estimate=SMALL,
        name="table_rows",
    )(step, gate_table, gate_slope)


def score_kernel(q, qt, k, kt, k_par, par, near_a, near_b, late_a, late_b, p_out, w_out, mid_out):
    tokens, features = q.shape
    edge = near_a.shape[0] // 4
    half = 2 * edge
    inner = tokens - 2 * edge
    first = tokens + 2 * half
    scaling = 1.0 / math.sqrt(HD)
    tm = lax.axis_index("tm")
    inside = (tm > 0) & (tm < lax.axis_size("tm") - 1)
    seen = jnp.where(inside, tokens + 2 * half + inner + half, tokens + 2 * half + inner)
    allowed = lax.broadcasted_iota(jnp.int32, (tokens, 2 * tokens + 2 * half), 1) < seen
    for head in range(features // HD):
        at = pl.ds(head * HD, HD)

        def ordered(own, par, i):
            rows = pl.ds(i * edge, edge)
            return jnp.concatenate(
                [
                    own[:, at],
                    par[pl.ds(0, edge), at],
                    par[pl.ds(tokens - edge, edge), at],
                    near_a[rows, at],
                    late_a[rows, at],
                    par[pl.ds(edge, inner), at],
                    near_b[rows, at],
                    late_b[rows, at],
                ],
                0,
            )

        keys, keys_t = ordered(k, k_par, 0), ordered(kt, par, 1)
        query, query_t = q[:, at], qt[:, at]
        raw = jnp.where(allowed, dot_nt(query, keys), -1e30)
        top = jnp.max(raw, axis=-1, keepdims=True)
        lifted = jnp.exp2((raw - top) * (scaling * LOG2E))
        probs = lifted * (1.0 / jnp.sum(lifted, axis=-1, keepdims=True))
        slopes = scaling * dot_nt(
            jnp.concatenate([query_t, query], 1), jnp.concatenate([keys, keys_t], 1)
        )
        centre = jnp.sum(probs * slopes, axis=-1, keepdims=True)
        probs_low = probs.astype(jnp.bfloat16)
        weights_t = (probs * (slopes - centre)).astype(jnp.bfloat16)
        p_out[head] = probs_low
        w_out[head] = weights_t
        part = probs_low[:, first : first + inner]
        mid_out[head, pl.ds(0, tokens), :] = jnp.concatenate([part, jnp.zeros_like(part)], 1)
        mid_out[head, pl.ds(tokens, tokens), :] = jnp.concatenate([weights_t[:, first : first + inner], part], 1)


def scores(*arrays):
    tokens, features = arrays[0].shape
    heads = features // HD
    keys = 2 * tokens + arrays[-1].shape[0]
    inner = tokens - arrays[-1].shape[0] // 2
    out = jax.ShapeDtypeStruct((heads, tokens, keys), jnp.bfloat16)
    mid = jax.ShapeDtypeStruct((heads, 2 * tokens, 2 * inner), jnp.bfloat16)
    return pl.pallas_call(
        score_kernel,
        out_shape=(out, out, mid),
        in_specs=[pl.BlockSpec(memory_space=pltpu.VMEM)] * len(arrays),
        out_specs=[pl.BlockSpec(memory_space=pltpu.VMEM)] * 3,
        compiler_params=pltpu.CompilerParams(vmem_limit_bytes=VMEM_LIMIT),
        cost_estimate=SCORES_COST,
        name="scores",
    )(*arrays)


def values_kernel(layout, p, w, own, mids, par, near_a, near_b, late_a, late_b, *rest):
    pieces = rest[: len(layout)]
    total, weight = rest[len(layout) :]
    tokens = p.shape[1]
    edge = near_a.shape[0] // 4
    half, inner = 2 * edge, tokens - 2 * edge
    tm, h, f = (lax.axis_index(axis) for axis in ("tm", "height", "fsdp"))
    for piece, (units, rows) in zip(pieces, layout):
        for i, unit in enumerate(units):
            start = 0
            if unit is not None:
                dh, df, dq = unit
                wide = weight.shape[0] // (lax.axis_size("height") * lax.axis_size("fsdp"))
                start = ((h ^ dh) * lax.axis_size("fsdp") + (f ^ df)) * wide
                if dq is not None:
                    start = start + ((tm & 3) ^ dq) * rows
                start = pl.multiple_of(start, 16)
            weight[pl.ds(start, rows), :] = piece[pl.ds(i * rows, rows), :]
    gap = jnp.zeros((inner, HD), jnp.bfloat16)
    for head in range(p.shape[0]):
        at = pl.ds(head * HD, HD)

        def ordered(i):
            halo = pl.ds(half + i * edge, edge)
            base = tokens + i * half
            return jnp.concatenate(
                [
                    own[pl.ds(base, edge), at],
                    mids[pl.ds(i * inner, inner), at],
                    own[pl.ds(base + edge, edge), at],
                    par[pl.ds(base, half), at],
                    near_a[halo, at],
                    late_a[halo, at],
                    gap,
                    near_b[halo, at],
                    late_b[halo, at],
                ],
                0,
            )

        values, values_t = ordered(0), ordered(1)
        probs = p[head]
        total[pl.ds(0, tokens), at] = jnp.dot(probs, values, preferred_element_type=jnp.float32)
        total[pl.ds(tokens, tokens), at] = jnp.dot(
            jnp.concatenate([w[head], probs], 1),
            jnp.concatenate([values, values_t], 0),
            preferred_element_type=jnp.float32,
        )


def values_known(probs, weights_t, values, pieces, layout, dout):
    tokens, features = probs.shape[1], values[0].shape[1]
    arrays = (probs, weights_t, *values, *pieces)
    return pl.pallas_call(
        lambda *refs: values_kernel(layout, *refs),
        out_shape=(
            jax.ShapeDtypeStruct((2 * tokens, features), jnp.float32),
            jax.ShapeDtypeStruct((dout, features), jnp.bfloat16),
        ),
        in_specs=[pl.BlockSpec(memory_space=pltpu.VMEM)] * len(arrays),
        out_specs=[pl.BlockSpec(memory_space=pltpu.VMEM)] * 2,
        compiler_params=pltpu.CompilerParams(vmem_limit_bytes=VMEM_LIMIT),
        cost_estimate=SMALL,
        name="values",
    )(*arrays)


def project_kernel(gate, slope, mid, total, weight, v_mid, out_p, out_t, attn):
    tokens = out_p.shape[0]
    for head in range(mid.shape[0]):
        at = pl.ds(head * HD, HD)
        rest = jnp.dot(mid[head], v_mid[:, at], preferred_element_type=jnp.float32)
        attn[:, at] = (total[:, at] + rest).astype(jnp.bfloat16)
    width = 256
    for first in range(0, weight.shape[0], width):
        cols = pl.ds(first, width)
        both = dot_nt(attn[...], weight[cols, :])
        main, main_t = both[:tokens], both[tokens:]
        gate_row, slope_row = gate[:, cols], slope[:, cols]
        out_p[:, cols] = (gate_row * main).astype(jnp.bfloat16)
        out_t[:, cols] = (gate_row * main_t + slope_row * main).astype(jnp.bfloat16)


def project(gate, slope, mid, total, weight, v_mid):
    rows, features = total.shape
    dout = weight.shape[0]
    out = jax.ShapeDtypeStruct((rows // 2, dout), jnp.bfloat16)
    return pl.pallas_call(
        project_kernel,
        out_shape=(out, out),
        in_specs=[pl.BlockSpec(memory_space=pltpu.VMEM)] * 6,
        scratch_shapes=[pltpu.VMEM((rows, features), jnp.bfloat16)],
        compiler_params=pltpu.CompilerParams(vmem_limit_bytes=VMEM_LIMIT),
        cost_estimate=SMALL,
        name="project",
    )(gate, slope, mid, total, weight, v_mid)


def local(
    query_primal,
    key_primal,
    value_primal,
    query_tangent,
    key_tangent,
    value_tangent,
    out_weight,
    gate_table,
    gate_slope,
    timestep,
):
    _, frames, rows, columns, features = query_primal.shape
    per_frame = rows * columns
    tokens = frames * per_frame
    flat = lambda x: x.reshape(tokens, features)
    q, qt, k, kt, v, vt = map(
        flat, (query_primal, query_tangent, key_primal, key_tangent, value_primal, value_tangent)
    )
    block = out_weight.T
    wide = block.shape[0]
    part = wide // 4
    fsdp = lax.axis_size("fsdp")
    in_quarters = (lax.axis_size("tm") % 4, lax.axis_size("height"), fsdp) == (0, 2, 4) and part % 16 == 0
    two = 2 * per_frame
    inner, last = tokens - two, tokens - per_frame
    ends = ((0, last), (last, 0))

    def own_parts(k, kt, v, vt):
        moves = [(1, 0, 0, 0, tokens)]
        for i, source in ((0, 2), (1, 3)):
            moves.append((source, 0, 0, tokens + i * two, per_frame))
            moves.append((source, last, 0, tokens + i * two + per_frame, per_frame))
            moves.append((source, per_frame, 1, inner * i, inner))
        for out, (odd, even) in ((2, ends[0]), (3, ends[1])):
            for source in range(4):
                moves.append((source, (even, odd), out, source * per_frame, per_frame))
        return gather_rows("own_parts", [tokens + 2 * two, 2 * inner, 2 * two, 2 * two], moves, [k, kt, v, vt], 58 * 1024 * 1024)

    def late_parts(k_par, par):
        moves = []
        for out, (odd, even) in ((0, ends[0]), (1, ends[1])):
            for i in range(2):
                moves.append((i, (even, odd), out, i * per_frame, per_frame))
                row = tuple(tokens + i * two + min(end, per_frame) for end in (even, odd))
                moves.append((1, row, out, (2 + i) * per_frame, per_frame))
        return gather_rows("late_parts", [2 * two, 2 * two], moves, [k_par, par])

    steps = {
        "k": ((), lambda: k),
        "kt": ((), lambda: kt),
        "v": ((), lambda: (v, vt)),
        "own_parts": (("k", "kt", "v"), lambda k, kt, v: own_parts(k, kt, *v)),
        "k_par": (("k",), lambda k: swap(k, "height", 1)),
        "par": (("own_parts",), lambda parts: swap(parts[0], "height", 1)),
        "v_mid": (("own_parts",), lambda parts: swap(parts[1], "height", 1)),
        "near_a": (("own_parts",), lambda parts: swap(parts[2], "tm", 1)),
        "near_b": (("own_parts",), lambda parts: swap_odd(parts[3], "tm")),
        "late_parts": (("k_par", "par"), late_parts),
        "late_a": (("late_parts",), lambda sides: swap(sides[0], "tm", 1)),
        "late_b": (("late_parts",), lambda sides: swap_odd(sides[1], "tm")),
        "scores": (
            ("k_par", "par", "near_a", "near_b", "late_a", "late_b"),
            lambda *arrays: scores(q, qt, k, kt, *arrays),
        ),
        "tables": ((), lambda: (timestep, gate_table, gate_slope)),
        "gates": (("tables",), lambda tables: table_rows(*tables)),
    }
    if in_quarters:
        mine = lax.axis_index("tm") & 3
        quarter = lambda which: lax.dynamic_slice_in_dim(block, which * part, part, 0)
        near = lambda group: [(dh, df, dq ^ 1) for dh, df, dq in group]
        cat = lambda *arrays: jnp.concatenate(arrays, 0)
        steps["own"] = ((), lambda: quarter(mine))
        steps["other"] = (("own",), lambda own: swap(own, "height", 1))
        steps["pair"] = (("own", "other"), cat)
        steps["half"] = (("pair",), lambda pair: cat(quarter(mine ^ 2), pair))
        steps["twos"] = (("pair",), lambda pair: swap(pair, "fsdp", 2))
        steps["ones"] = (("half",), lambda half: swap(half, "fsdp", 1))
        steps["threes"] = (("twos",), lambda twos: swap(twos, "fsdp", 1))
        steps["other_x"] = (("other",), lambda other: swap(other, "tm", 2))
        steps["cross"] = (("ones", "twos"), lambda ones, twos: swap(cat(ones[2 * part :], twos), "tm", 2))
        steps["cross_threes"] = (("threes",), lambda threes: swap(threes, "tm", 2))
        steps["mine"] = (("other", "ones", "twos", "threes", "other_x", "cross", "cross_threes"), cat)
        units = [(1, 0, 0), (0, 1, 2), (0, 1, 0), (1, 1, 0), (0, 2, 0), (1, 2, 0), (0, 3, 0), (1, 3, 0)]
        units += [(1, 0, 2), (1, 1, 2), (0, 2, 2), (1, 2, 2), (0, 3, 2), (1, 3, 2)]
        steps["near"] = (("mine",), lambda mine: swap(mine, "tm", 1))
        pieces = ("mine", "near")
        layout = [([(0, 0, None)], wide), (units, part), (near(units), part)]
        order = ORDER
    else:
        steps["weight"] = ((), lambda: lax.all_gather(block, ("height", "fsdp"), axis=0, tiled=True))
        pieces, layout, order = ("weight",), [([None], gate_table.shape[1])], {}
    known = {}

    def get(name):
        if name not in known:
            takes, make = steps[name]
            arrays = [get(take) for take in takes]
            first = [get(step) for step in order.get(name, ())]
            if first:
                arrays = lax.optimization_barrier((arrays, first))[0]
            known[name] = make(*arrays)
        return known[name]

    probs, weights_t, mid = get("scores")
    own, middle, _, _ = get("own_parts")
    known_values = (own, middle, *(get(name) for name in ("par", "near_a", "near_b", "late_a", "late_b")))
    parts = ([block] if in_quarters else []) + [get(piece) for piece in pieces]
    total, weight = values_known(probs, weights_t, known_values, parts, layout, gate_table.shape[1])
    out_p, out_t = project(*get("gates"), mid, total, weight, get("v_mid"))
    shape = query_primal.shape[:-1] + (out_p.shape[1],)
    return out_p.reshape(shape), out_t.reshape(shape)


def solution(mesh):
    token_spec = P("fsdp", "tm", "height", None, None)
    in_specs = (token_spec,) * 6 + (P(None, ("height", "fsdp")), P(), P(), P("fsdp"))
    return jax.shard_map(
        local, mesh=mesh, in_specs=in_specs, out_specs=(token_spec, token_spec), check_vma=False
    )
```

time: 93.2 us -> 60.1 us (0.64)
  the two profiles are of different devices: /device:TPU:9 before, /device:TPU:1 now
where the time goes in v2:
time: 60.1 us; the launch traced here: 59.9 us
  waiting for transfers between devices  24.3 us (40%)
  starting transfers between devices  22.1 us (37%)
  Pallas kernels  10.6 us (18%)
  between operations  1.59 us (3%)
  local copies, waits for them, and re-layouts  1.26 us (2%)
    ppermute x13, waiting for transfers between devices, swap(): return lax.ppermute(value, axis, pairs)  21.5 us
    ppermute x13, starting transfers between devices, swap(): return lax.ppermute(value, axis, pairs)  14.2 us
    ppermute x2, starting transfers between devices, swap_odd(): return lax.ppermute(value, axis, pairs)  7.9 us
    pallas_call x2, Pallas kernels, gather_rows(): pl.pallas_call(kernel, out_shape=[jax.ShapeDtypeStruct((n, features), sou...  4.07 us
    ppermute x2, waiting for transfers between devices, swap_odd(): return lax.ppermute(value, axis, pairs)  2.72 us
    pallas_call x1, Pallas kernels, scores(): pl.pallas_call(score_kernel, out_shape=(out, out, mid), in_specs=[pl.Bloc...  2.6 us
    pallas_call x1, Pallas kernels, project(): pl.pallas_call(project_kernel, out_shape=(out, out), in_specs=[pl.BlockSp...  2.5 us
    pallas_call x1, Pallas kernels, values_known(): pl.pallas_call(lambda *refs: values_kernel(layout, *refs), out_shape=(jax...  1.39 us
  transfers between devices with their start and end apart: 15, of which 6 were waited for; matrix products, arithmetic and copies ran while one was open for 0% of the time, Pallas kernels for 11%

profile of v2, /device:TPU:1, one launch (start us, length us, event | category | flops | bytes accessed | tf_op | source)
XLA Modules:
  0.0 59.9 jit_solution(369929594369339354)
XLA Ops:
  0.7 1.1 %dynamic-slice_bitcast_fusion = (bf16[48,1536]{1,0:T(8,128)(2,1)S(1)}, bf16[48,1536]{1,0:T(8,128)(2,1)S(1)}) fusion(bf16[1536,192]{0,1:T(8,128)(2,1)} %param.16, s32[]{:T(128)S(6)} %select_n.7, s32[]{:T(128)S(6)} %select_n.6), kind=kLoop, calls=%fused_computation.3 | loop fusion | bytes 589832 | tf_op jit(solution)/shard_map/dynamic_slice | solution.py:337
  1.7 2.1 %collective-permute-start = (bf16[48,1536]{1,0:T(8,128)(2,1)S(1)}, bf16[48,1536]{1,0:T(8,128)(2,1)S(1)}, u32[]{:S(2)}, u32[]{:S(2)}) collective-permute-start(bf16[48,1536]{1,0:T(8,128)(2,1)S(1)} %get-tuple-element.57), channel_id=1, source_target_pairs={{0,4},{4,0},{1,5},{5,1},{2,6},{6,2},{3,7},{7,3},{8,12},{12,8},{9,1... | collective-permute-start | bytes 442376 | tf_op jit(solution)/shard_map/ppermute | solution.py:30
  3.8 3.0 %own_parts.1 = (bf16[256,1536]{1,0:T(8,128)(2,1)}, bf16[128,1536]{1,0:T(8,128)(2,1)}, bf16[128,1536]{1,0:T(8,128)(2,1)}, bf16[128,1536]{1,0:T(8,128)(2,1)}) custom-call(bf16[128,1536]{1,0:T(8,128)(2,1)} %bitcast.14, bf16[128,1536]{1,0:T(8,128)(2,1)} %bitcast.17, bf16[128,1536]{1,0:T(8,128)(2,1)} %bitcast.21, bf16[128,1536]{1,0:T(8,128)(2,1)} %bitcast.22), custom_call_target="tpu_custom_call" | custom-call | flops 1 | bytes 1 | tf_op jit(solution)/shard_map/own_parts/pallas_call | solution.py:68
  6.8 0.6 %collective-permute-done = bf16[48,1536]{1,0:T(8,128)(2,1)S(1)} collective-permute-done((bf16[48,1536]{1,0:T(8,128)(2,1)S(1)}, bf16[48,1536]{1,0:T(8,128)(2,1)S(1)}, u32[]{:S(2)}, u32[]{:S(2)}) %collective-permute-start) | collective-permute-done | bytes 147488 | tf_op jit(solution)/shard_map/ppermute | solution.py:30
  7.5 1.3 %collective-permute-start.9 = (bf16[144,1536]{1,0:T(8,128)(2,1)S(1)}, bf16[144,1536]{1,0:T(8,128)(2,1)S(1)}, u32[]{:S(2)}, u32[]{:S(2)}) collective-permute-start(bf16[144,1536]{1,0:T(8,128)(2,1)S(1)} %pad_maximum_fusion), channel_id=1, source_target_pairs={{0,1},{1,0},{2,3},{3,2},{4,5},{5,4},{6,7},{7,6},{8,9},{9,8},{10,11... | collective-permute-start | bytes 1327112 | tf_op jit(solution)/shard_map/ppermute | solution.py:30
  8.8 1.2 %collective-permute-start.2 = (bf16[128,1536]{1,0:T(8,128)(2,1)S(1)}, bf16[128,1536]{1,0:T(8,128)(2,1)S(1)}, u32[]{:S(2)}, u32[]{:S(2)}) collective-permute-start(bf16[128,1536]{1,0:T(8,128)(2,1)S(1)} %bitcast.15), channel_id=1, source_target_pairs={{0,4},{4,0},{1,5},{5,1},{2,6},{6,2},{3,7},{7,3},{8,12},{12,8},{9,1... | collective-permute-start | bytes 1179656 | tf_op jit(solution)/shard_map/ppermute | solution.py:30
  10.0 5.1 %collective-permute-start.5 = (bf16[128,1536]{1,0:T(8,128)(2,1)}, bf16[128,1536]{1,0:T(8,128)(2,1)S(1)}, u32[]{:S(2)}, u32[]{:S(2)}) collective-permute-start(bf16[128,1536]{1,0:T(8,128)(2,1)} %get-tuple-element.32), channel_id=1, source_target_pairs={{8,16},{16,8},{9,17},{17,9},{10,18},{18,10},{11,19},{19,11},{12,20... | collective-permute-start | bytes 1179656 | tf_op jit(solution)/shard_map/ppermute | solution.py:37
  15.1 2.4 %collective-permute-start.1 = (bf16[96,1536]{1,0:T(8,128)(2,1)S(1)}, bf16[96,1536]{1,0:T(8,128)(2,1)S(1)}, u32[]{:S(2)}, u32[]{:S(2)}) collective-permute-start(bf16[96,1536]{1,0:T(8,128)(2,1)S(1)} %pad_maximum_fusion.2), channel_id=1, source_target_pairs={{0,2},{1,3},{2,0},{3,1},{4,6},{5,7},{6,4},{7,5},{8,10},{9,11},{10,... | collective-permute-start | bytes 884744 | tf_op jit(solution)/shard_map/ppermute | solution.py:30
  17.5 0.2 collective-permute-start.3
  17.7 2.6 %collective-permute-start.4 = (bf16[128,1536]{1,0:T(8,128)(2,1)}, bf16[128,1536]{1,0:T(8,128)(2,1)S(1)}, u32[]{:S(2)}, u32[]{:S(2)}) collective-permute-start(bf16[128,1536]{1,0:T(8,128)(2,1)} %get-tuple-element.31), channel_id=1, source_target_pairs={{0,8},{8,0},{16,24},{24,16},{1,9},{9,1},{17,25},{25,17},{2,10},{10... | collective-permute-start | bytes 1179656 | tf_op jit(solution)/shard_map/ppermute | solution.py:30
  20.3 9.0 %collective-permute-done.1 = bf16[96,1536]{1,0:T(8,128)(2,1)S(1)} collective-permute-done((bf16[96,1536]{1,0:T(8,128)(2,1)S(1)}, bf16[96,1536]{1,0:T(8,128)(2,1)S(1)}, u32[]{:S(2)}, u32[]{:S(2)}) %collective-permute-start.1) | collective-permute-done | bytes 294944 | tf_op jit(solution)/shard_map/ppermute | solution.py:30
  29.4 1.5 %collective-permute-start.11 = (bf16[144,1536]{1,0:T(8,128)(2,1)S(1)}, bf16[144,1536]{1,0:T(8,128)(2,1)S(1)}, u32[]{:S(2)}, u32[]{:S(2)}) collective-permute-start(bf16[144,1536]{1,0:T(8,128)(2,1)S(1)} %pad_maximum_fusion.1), channel_id=1, source_target_pairs={{0,16},{8,24},{16,0},{24,8},{1,17},{9,25},{17,1},{25,9},{2,18},{10... | collective-permute-start | bytes 1327112 | tf_op jit(solution)/shard_map/ppermute | solution.py:30
  31.0 6.9 %collective-permute-done.6 = bf16[96,1536]{1,0:T(8,128)(2,1)S(1)} collective-permute-done((bf16[96,1536]{1,0:T(8,128)(2,1)S(1)}, bf16[96,1536]{1,0:T(8,128)(2,1)S(1)}, u32[]{:S(2)}, u32[]{:S(2)}) %collective-permute-start.6) | collective-permute-done | bytes 294944 | tf_op jit(solution)/shard_map/ppermute | solution.py:30
  38.1 1.5 %collective-permute-start.12 = (bf16[96,1536]{1,0:T(8,128)(2,1)S(1)}, bf16[96,1536]{1,0:T(8,128)(2,1)S(1)}, u32[]{:S(2)}, u32[]{:S(2)}) collective-permute-start(bf16[96,1536]{1,0:T(8,128)(2,1)S(1)} %collective-permute-done.6), channel_id=1, source_target_pairs={{0,16},{8,24},{16,0},{24,8},{1,17},{9,25},{17,1},{25,9},{2,18},{10... | collective-permute-start | bytes 884744 | tf_op jit(solution)/shard_map/ppermute | solution.py:30
  39.6 1.1 %late_parts.1 = (bf16[128,1536]{1,0:T(8,128)(2,1)S(1)}, bf16[128,1536]{1,0:T(8,128)(2,1)S(1)}) custom-call(bf16[128,1536]{1,0:T(8,128)(2,1)S(1)} %collective-permute-done.2.refs_0_.k_par, bf16[256,1536]{1,0:T(8,128)(2,1)S(1)} %collective-permute-done.3.refs_1_.par.refs_4_), custom_call_target="tpu_custom_call" | custom-call | flops 1 | bytes 1 | tf_op jit(solution)/shard_map/late_parts/pallas_call | solution.py:68
  40.8 0.6 collective-permute-start.7
  41.3 1.5 %collective-permute-done.11 = bf16[144,1536]{1,0:T(8,128)(2,1)S(1)} collective-permute-done((bf16[144,1536]{1,0:T(8,128)(2,1)S(1)}, bf16[144,1536]{1,0:T(8,128)(2,1)S(1)}, u32[]{:S(2)}, u32[]{:S(2)}) %collective-permute-start.11) | collective-permute-done | bytes 442400 | tf_op jit(solution)/shard_map/ppermute | solution.py:30
  42.9 2.8 %collective-permute-start.8 = (bf16[128,1536]{1,0:T(8,128)(2,1)S(1)}, bf16[128,1536]{1,0:T(8,128)(2,1)S(1)}, u32[]{:S(2)}, u32[]{:S(2)}) collective-permute-start(bf16[128,1536]{1,0:T(8,128)(2,1)S(1)} %get-tuple-element.44), channel_id=1, source_target_pairs={{8,16},{16,8},{9,17},{17,9},{10,18},{18,10},{11,19},{19,11},{12,20... | collective-permute-start | bytes 1179656 | tf_op jit(solution)/shard_map/ppermute | solution.py:37
  45.7 3.5 %collective-permute-done.12 = bf16[96,1536]{1,0:T(8,128)(2,1)S(1)} collective-permute-done((bf16[96,1536]{1,0:T(8,128)(2,1)S(1)}, bf16[96,1536]{1,0:T(8,128)(2,1)S(1)}, u32[]{:S(2)}, u32[]{:S(2)}) %collective-permute-start.12) | collective-permute-done | bytes 294944 | tf_op jit(solution)/shard_map/ppermute | solution.py:30
  49.2 0.7 %collective-permute-start.14 = (bf16[672,1536]{1,0:T(8,128)(2,1)S(1)}, bf16[672,1536]{1,0:T(8,128)(2,1)S(1)}, u32[]{:S(2)}, u32[]{:S(2)}) collective-permute-start(bf16[672,1536]{1,0:T(8,128)(2,1)S(1)} %constant_dynamic-update-slice_fusion.refs_10_), channel_id=1, source_target_pairs={{0,8},{8,0},{16,24},{24,16},{1,9},{9,1},{17,25},{25,17},{2,10},{10... | collective-permute-start | bytes 6193160 | tf_op jit(solution)/shard_map/ppermute | solution.py:30
  50.6 2.7 %collective-permute-done.8.late_b.refs_8_ = bf16[128,1536]{1,0:T(8,128)(2,1)S(1)} collective-permute-done((bf16[128,1536]{1,0:T(8,128)(2,1)S(1)}, bf16[128,1536]{1,0:T(8,128)(2,1)S(1)}, u32[]{:S(2)}, u32[]{:S(2)}) %collective-permute-start.8) | collective-permute-done | bytes 393248 | tf_op jit(solution)/shard_map/ppermute | solution.py:37
  53.3 2.6 %scores.1 = (bf16[12,128,384]{2,1,0:T(8,128)(2,1)S(1)}, bf16[12,128,384]{2,1,0:T(8,128)(2,1)S(1)}, bf16[12,256,128]{2,1,0:T(8,128)(2,1)S(1)}) custom-call(bf16[128,1536]{1,0:T(8,128)(2,1)S(1)} %bitcast.19, bf16[128,1536]{1,0:T(8,128)(2,1)S(1)} %bitcast.20, bf16[128,1536]{1,0:T(8,128)(2,1)S(1)} %bitcast.16, bf16[128,1536]{1,0:T(8,128)(2,1)S(1)} %bitcast.18, ...), custom_call_target="tpu_custom_call" | custom-call | flops 20000000000 | bytes 1 | tf_op jit(solution)/shard_map/scores/pallas_call | solution.py:158
  56.0 1.4 %values.1 = (f32[256,1536]{1,0:T(8,128)S(1)}, bf16[1536,1536]{1,0:T(8,128)(2,1)S(1)}) custom-call(bf16[12,128,384]{2,1,0:T(8,128)(2,1)S(1)} %get-tuple-element.46.refs_0_, bf16[12,128,384]{2,1,0:T(8,128)(2,1)S(1)} %get-tuple-element.47.refs_1_, bf16[256,1536]{1,0:T(8,128)(2,1)S(1)} %copy-done.1, bf16[128,1536]{1,0:T(8,128)(2,1)S(1)} %copy-done.6, ...), custom_call_target="tpu_custom_call" | custom-call | flops 1 | bytes 1 | tf_op jit(solution)/shard_map/values/pallas_call | solution.py:222
  57.4 2.5 %project.1 = (bf16[128,1536]{1,0:T(8,128)(2,1)}, bf16[128,1536]{1,0:T(8,128)(2,1)}) custom-call(f32[1,1536]{1,0:T(1,128)S(1)} %get-tuple-element.37.gate, f32[1,1536]{1,0:T(1,128)S(1)} %get-tuple-element.38.slope, bf16[12,256,128]{2,1,0:T(8,128)(2,1)S(1)} %get-tuple-element.45.mid, f32[256,1536]{1,0:T(8,128)S(1)} %get-tuple-element.52.total, ...), custom_call_target="tpu_custom_call" | custom-call | flops 1 | bytes 1 | tf_op jit(solution)/shard_map/project/pallas_call | solution.py:256
  (42 shorter events, 0.5 us)
Async XLA Ops:
  0.6 8.1 %copy-start.4 = (bf16[1,4,4,8,1536]{4,3,2,1,0:T(8,128)(2,1)S(1)}, bf16[1,4,4,8,1536]{4,3,2,1,0:T(8,128)(2,1)}, u32[]{:S(2)}) copy-start(bf16[1,4,4,8,1536]{4,3,2,1,0:T(8,128)(2,1)} %param.11) | copy-start | bytes 1179652
  1.7 5.7 %collective-permute-start = (bf16[48,1536]{1,0:T(8,128)(2,1)S(1)}, bf16[48,1536]{1,0:T(8,128)(2,1)S(1)}, u32[]{:S(2)}, u32[]{:S(2)}) collective-permute-start(bf16[48,1536]{1,0:T(8,128)(2,1)S(1)} %get-tuple-element.57), channel_id=1, source_target_pairs={{0,4},{4,0},{1,5},{5,1},{2,6},{6,2},{3,7},{7,3},{8,12},{12,8},{9,1... | collective-permute-start | bytes 442376 | tf_op jit(solution)/shard_map/ppermute | solution.py:30
  7.4 30.5 %copy-start.6 = (bf16[128,1536]{1,0:T(8,128)(2,1)S(1)}, bf16[128,1536]{1,0:T(8,128)(2,1)}, u32[]{:S(2)}) copy-start(bf16[128,1536]{1,0:T(8,128)(2,1)} %get-tuple-element.50.refs_3_) | copy-start | bytes 1179652
  7.5 21.8 %collective-permute-start.9 = (bf16[144,1536]{1,0:T(8,128)(2,1)S(1)}, bf16[144,1536]{1,0:T(8,128)(2,1)S(1)}, u32[]{:S(2)}, u32[]{:S(2)}) collective-permute-start(bf16[144,1536]{1,0:T(8,128)(2,1)S(1)} %pad_maximum_fusion), channel_id=1, source_target_pairs={{0,1},{1,0},{2,3},{3,2},{4,5},{5,4},{6,7},{7,6},{8,9},{9,8},{10,11... | collective-permute-start | bytes 1327112 | tf_op jit(solution)/shard_map/ppermute | solution.py:30
  8.8 9.0 %collective-permute-start.2 = (bf16[128,1536]{1,0:T(8,128)(2,1)S(1)}, bf16[128,1536]{1,0:T(8,128)(2,1)S(1)}, u32[]{:S(2)}, u32[]{:S(2)}) collective-permute-start(bf16[128,1536]{1,0:T(8,128)(2,1)S(1)} %bitcast.15), channel_id=1, source_target_pairs={{0,4},{4,0},{1,5},{5,1},{2,6},{6,2},{3,7},{7,3},{8,12},{12,8},{9,1... | collective-permute-start | bytes 1179656 | tf_op jit(solution)/shard_map/ppermute | solution.py:30
  10.0 19.3 %collective-permute-start.5 = (bf16[128,1536]{1,0:T(8,128)(2,1)}, bf16[128,1536]{1,0:T(8,128)(2,1)S(1)}, u32[]{:S(2)}, u32[]{:S(2)}) collective-permute-start(bf16[128,1536]{1,0:T(8,128)(2,1)} %get-tuple-element.32), channel_id=1, source_target_pairs={{8,16},{16,8},{9,17},{17,9},{10,18},{18,10},{11,19},{19,11},{12,20... | collective-permute-start | bytes 1179656 | tf_op jit(solution)/shard_map/ppermute | solution.py:37
  15.1 14.2 %collective-permute-start.1 = (bf16[96,1536]{1,0:T(8,128)(2,1)S(1)}, bf16[96,1536]{1,0:T(8,128)(2,1)S(1)}, u32[]{:S(2)}, u32[]{:S(2)}) collective-permute-start(bf16[96,1536]{1,0:T(8,128)(2,1)S(1)} %pad_maximum_fusion.2), channel_id=1, source_target_pairs={{0,2},{1,3},{2,0},{3,1},{4,6},{5,7},{6,4},{7,5},{8,10},{9,11},{10,... | collective-permute-start | bytes 884744 | tf_op jit(solution)/shard_map/ppermute | solution.py:30
  17.5 22.1 %collective-permute-start.3 = (bf16[256,1536]{1,0:T(8,128)(2,1)}, bf16[256,1536]{1,0:T(8,128)(2,1)S(1)}, u32[]{:S(2)}, u32[]{:S(2)}) collective-permute-start(bf16[256,1536]{1,0:T(8,128)(2,1)} %get-tuple-element.29.refs_2_), channel_id=1, source_target_pairs={{0,4},{4,0},{1,5},{5,1},{2,6},{6,2},{3,7},{7,3},{8,12},{12,8},{9,1... | collective-permute-start | bytes 2359304 | tf_op jit(solution)/shard_map/ppermute | solution.py:30
  17.7 32.9 %collective-permute-start.4 = (bf16[128,1536]{1,0:T(8,128)(2,1)}, bf16[128,1536]{1,0:T(8,128)(2,1)S(1)}, u32[]{:S(2)}, u32[]{:S(2)}) collective-permute-start(bf16[128,1536]{1,0:T(8,128)(2,1)} %get-tuple-element.31), channel_id=1, source_target_pairs={{0,8},{8,0},{16,24},{24,16},{1,9},{9,1},{17,25},{25,17},{2,10},{10... | collective-permute-start | bytes 1179656 | tf_op jit(solution)/shard_map/ppermute | solution.py:30
  29.3 8.8 %collective-permute-start.10 = (bf16[48,1536]{1,0:T(8,128)(2,1)S(1)}, bf16[48,1536]{1,0:T(8,128)(2,1)S(1)}, u32[]{:S(2)}, u32[]{:S(2)}) collective-permute-start(bf16[48,1536]{1,0:T(8,128)(2,1)S(1)} %collective-permute-done), channel_id=1, source_target_pairs={{0,16},{8,24},{16,0},{24,8},{1,17},{9,25},{17,1},{25,9},{2,18},{10... | collective-permute-start | bytes 442376 | tf_op jit(solution)/shard_map/ppermute | solution.py:30
  29.3 8.6 %collective-permute-start.6 = (bf16[96,1536]{1,0:T(8,128)(2,1)S(1)}, bf16[96,1536]{1,0:T(8,128)(2,1)S(1)}, u32[]{:S(2)}, u32[]{:S(2)}) collective-permute-start(bf16[96,1536]{1,0:T(8,128)(2,1)S(1)} %collective-permute-done.1), channel_id=1, source_target_pairs={{0,1},{1,0},{2,3},{3,2},{4,5},{5,4},{6,7},{7,6},{8,9},{9,8},{10,11... | collective-permute-start | bytes 884744 | tf_op jit(solution)/shard_map/ppermute | solution.py:30
  29.4 13.5 %collective-permute-start.11 = (bf16[144,1536]{1,0:T(8,128)(2,1)S(1)}, bf16[144,1536]{1,0:T(8,128)(2,1)S(1)}, u32[]{:S(2)}, u32[]{:S(2)}) collective-permute-start(bf16[144,1536]{1,0:T(8,128)(2,1)S(1)} %pad_maximum_fusion.1), channel_id=1, source_target_pairs={{0,16},{8,24},{16,0},{24,8},{1,17},{9,25},{17,1},{25,9},{2,18},{10... | collective-permute-start | bytes 1327112 | tf_op jit(solution)/shard_map/ppermute | solution.py:30
  30.9 19.6 %copy-start.2 = (f32[64,1536]{1,0:T(8,128)S(1)}, f32[64,1536]{1,0:T(8,128)}, u32[]{:S(2)}) copy-start(f32[64,1536]{1,0:T(8,128)} %gate) | copy-start | bytes 1179652
  31.0 19.6 %copy-start.3 = (f32[64,1536]{1,0:T(8,128)S(1)}, f32[64,1536]{1,0:T(8,128)}, u32[]{:S(2)}) copy-start(f32[64,1536]{1,0:T(8,128)} %slope) | copy-start | bytes 1179652
  31.0 22.3 %copy-start.5 = (bf16[1,4,4,8,1536]{4,3,2,1,0:T(8,128)(2,1)S(1)}, bf16[1,4,4,8,1536]{4,3,2,1,0:T(8,128)(2,1)}, u32[]{:S(2)}) copy-start(bf16[1,4,4,8,1536]{4,3,2,1,0:T(8,128)(2,1)} %param.14) | copy-start | bytes 1179652
  31.0 22.3 %copy-start.7 = (bf16[1,4,4,8,1536]{4,3,2,1,0:T(8,128)(2,1)S(1)}, bf16[1,4,4,8,1536]{4,3,2,1,0:T(8,128)(2,1)}, u32[]{:S(2)}) copy-start(bf16[1,4,4,8,1536]{4,3,2,1,0:T(8,128)(2,1)} %param.10) | copy-start | bytes 1179652
  31.0 22.3 %copy-start.8 = (bf16[1,4,4,8,1536]{4,3,2,1,0:T(8,128)(2,1)S(1)}, bf16[1,4,4,8,1536]{4,3,2,1,0:T(8,128)(2,1)}, u32[]{:S(2)}) copy-start(bf16[1,4,4,8,1536]{4,3,2,1,0:T(8,128)(2,1)} %param.13) | copy-start | bytes 1179652
  37.9 11.3 %collective-permute-start.13 = (bf16[128,1536]{1,0:T(8,128)(2,1)S(1)}, bf16[128,1536]{1,0:T(8,128)(2,1)S(1)}, u32[]{:S(2)}, u32[]{:S(2)}) collective-permute-start(bf16[128,1536]{1,0:T(8,128)(2,1)S(1)} %copy-done.6), channel_id=1, source_target_pairs={{0,4},{4,0},{1,5},{5,1},{2,6},{6,2},{3,7},{7,3},{8,12},{12,8},{9,1... | collective-permute-start | bytes 1179656 | tf_op jit(solution)/shard_map/ppermute | solution.py:30
  38.1 11.1 %collective-permute-start.12 = (bf16[96,1536]{1,0:T(8,128)(2,1)S(1)}, bf16[96,1536]{1,0:T(8,128)(2,1)S(1)}, u32[]{:S(2)}, u32[]{:S(2)}) collective-permute-start(bf16[96,1536]{1,0:T(8,128)(2,1)S(1)} %collective-permute-done.6), channel_id=1, source_target_pairs={{0,16},{8,24},{16,0},{24,8},{1,17},{9,25},{17,1},{25,9},{2,18},{10... | collective-permute-start | bytes 884744 | tf_op jit(solution)/shard_map/ppermute | solution.py:30
  40.8 9.8 %collective-permute-start.7 = (bf16[128,1536]{1,0:T(8,128)(2,1)S(1)}, bf16[128,1536]{1,0:T(8,128)(2,1)S(1)}, u32[]{:S(2)}, u32[]{:S(2)}) collective-permute-start(bf16[128,1536]{1,0:T(8,128)(2,1)S(1)} %get-tuple-element.43), channel_id=1, source_target_pairs={{0,8},{8,0},{16,24},{24,16},{1,9},{9,1},{17,25},{25,17},{2,10},{10... | collective-permute-start | bytes 1179656 | tf_op jit(solution)/shard_map/ppermute | solution.py:30
  42.9 10.4 %collective-permute-start.8 = (bf16[128,1536]{1,0:T(8,128)(2,1)S(1)}, bf16[128,1536]{1,0:T(8,128)(2,1)S(1)}, u32[]{:S(2)}, u32[]{:S(2)}) collective-permute-start(bf16[128,1536]{1,0:T(8,128)(2,1)S(1)} %get-tuple-element.44), channel_id=1, source_target_pairs={{8,16},{16,8},{9,17},{17,9},{10,18},{18,10},{11,19},{19,11},{12,20... | collective-permute-start | bytes 1179656 | tf_op jit(solution)/shard_map/ppermute | solution.py:37
  49.2 6.7 %collective-permute-start.14 = (bf16[672,1536]{1,0:T(8,128)(2,1)S(1)}, bf16[672,1536]{1,0:T(8,128)(2,1)S(1)}, u32[]{:S(2)}, u32[]{:S(2)}) collective-permute-start(bf16[672,1536]{1,0:T(8,128)(2,1)S(1)} %constant_dynamic-update-slice_fusion.refs_10_), channel_id=1, source_target_pairs={{0,8},{8,0},{16,24},{24,16},{1,9},{9,1},{17,25},{25,17},{2,10},{10... | collective-permute-start | bytes 6193160 | tf_op jit(solution)/shard_map/ppermute | solution.py:30
  53.3 2.6 %copy-start = (bf16[1536,192]{0,1:T(8,128)(2,1)S(1)}, bf16[1536,192]{0,1:T(8,128)(2,1)}, u32[]{:S(2)}) copy-start(bf16[1536,192]{0,1:T(8,128)(2,1)} %param.16) | copy-start | bytes 1769476
  53.3 2.6 %copy-start.1 = (bf16[256,1536]{1,0:T(8,128)(2,1)S(1)}, bf16[256,1536]{1,0:T(8,128)(2,1)}, u32[]{:S(2)}) copy-start(bf16[256,1536]{1,0:T(8,128)(2,1)} %get-tuple-element.29.refs_2_) | copy-start | bytes 2359300

commit v3 on v2

--- a/solution.py
+++ b/solution.py
@@ -11,13 +11,13 @@
 ORDER = {
     "k_par": ["own"],
     "twos": ["own_parts"],
-    "half": ["own_parts"],
     "threes": ["k_par"],
-    "cross": ["near_b"],
-    "v_mid": ["threes"],
+    "v_mid": ["k_par"],
     "near": ["v_mid"],
     "gates": ["twos"],
     "late_parts": ["threes"],
+    "near_b": ["other_x"],
+    "near_a": ["near_b"],
 }
 LOG2E = 1.4426950408889634
 VMEM_LIMIT = 24 * 1024 * 1024
@@ -30,7 +30,20 @@
     return lax.ppermute(value, axis, pairs)
 
 
-def swap_odd(value, axis):
+def swap_odd(value, ends_meet):
+    tiles, samples = lax.axis_size("tm"), lax.axis_size("fsdp")
+    pairs = []
+    for tile in range(tiles):
+        other = tile + 1 if tile % 2 else tile - 1
+        for sample in range(samples):
+            target = (other % tiles, sample)
+            if not 0 <= other < tiles and not ends_meet:
+                target = (tile, sample ^ 1)
+            pairs.append((tile * samples + sample, target[0] * samples + target[1]))
+    return lax.ppermute(value, ("tm", "fsdp"), pairs)
+
+
+def swap_odd_alone(value, axis):
     pairs = []
     for low in range(1, lax.axis_size(axis) - 1, 2):
         pairs += [(low, low + 1), (low + 1, low)]
@@ -99,12 +112,11 @@
     )(step, gate_table, gate_slope)
 
 
-def score_kernel(q, qt, k, kt, k_par, par, near_a, near_b, late_a, late_b, p_out, w_out, mid_out):
+def score_kernel(q, qt, k, kt, k_par, par, near_a, near_b, late_a, late_b, p_out, w_out):
     tokens, features = q.shape
     edge = near_a.shape[0] // 4
     half = 2 * edge
     inner = tokens - 2 * edge
-    first = tokens + 2 * half
     scaling = 1.0 / math.sqrt(HD)
     tm = lax.axis_index("tm")
     inside = (tm > 0) & (tm < lax.axis_size("tm") - 1)
@@ -143,35 +155,61 @@
         weights_t = (probs * (slopes - centre)).astype(jnp.bfloat16)
         p_out[head] = probs_low
         w_out[head] = weights_t
-        part = probs_low[:, first : first + inner]
-        mid_out[head, pl.ds(0, tokens), :] = jnp.concatenate([part, jnp.zeros_like(part)], 1)
-        mid_out[head, pl.ds(tokens, tokens), :] = jnp.concatenate([weights_t[:, first : first + inner], part], 1)
 
 
 def scores(*arrays):
     tokens, features = arrays[0].shape
     heads = features // HD
     keys = 2 * tokens + arrays[-1].shape[0]
-    inner = tokens - arrays[-1].shape[0] // 2
     out = jax.ShapeDtypeStruct((heads, tokens, keys), jnp.bfloat16)
-    mid = jax.ShapeDtypeStruct((heads, 2 * tokens, 2 * inner), jnp.bfloat16)
     return pl.pallas_call(
         score_kernel,
-        out_shape=(out, out, mid),
+        out_shape=(out, out),
         in_specs=[pl.BlockSpec(memory_space=pltpu.VMEM)] * len(arrays),
-        out_specs=[pl.BlockSpec(memory_space=pltpu.VMEM)] * 3,
+        out_specs=[pl.BlockSpec(memory_space=pltpu.VMEM)] * 2,
         compiler_params=pltpu.CompilerParams(vmem_limit_bytes=VMEM_LIMIT),
         cost_estimate=SCORES_COST,
         name="scores",
     )(*arrays)
 
 
-def values_kernel(layout, p, w, own, mids, par, near_a, near_b, late_a, late_b, *rest):
+def finish_kernel(layout, gate, slope, p, w, own, mids, par, near_a, near_b, late_a, late_b, v_mid, *rest):
     pieces = rest[: len(layout)]
-    total, weight = rest[len(layout) :]
+    out_p, out_t, weight, attn, rounded, sems = rest[len(layout) :]
     tokens = p.shape[1]
     edge = near_a.shape[0] // 4
     half, inner = 2 * edge, tokens - 2 * edge
+    for head in range(p.shape[0]):
+        at = pl.ds(head * HD, HD)
+
+        def ordered(i):
+            halo = pl.ds(half + i * edge, edge)
+            base = tokens + i * half
+            return jnp.concatenate(
+                [
+                    own[pl.ds(base, edge), at],
+                    mids[pl.ds(i * inner, inner), at],
+                    own[pl.ds(base + edge, edge), at],
+                    par[pl.ds(base, half), at],
+                    near_a[halo, at],
+                    late_a[halo, at],
+                    v_mid[pl.ds(i * inner, inner), at],
+                    near_b[halo, at],
+                    late_b[halo, at],
+                ],
+                0,
+            )
+
+        values, values_t = ordered(0), ordered(1)
+        probs = p[head]
+        primal = jnp.dot(probs, values, preferred_element_type=jnp.float32)
+        tangent = jnp.dot(
+            jnp.concatenate([w[head], probs], 1),
+            jnp.concatenate([values, values_t], 0),
+            preferred_element_type=jnp.float32,
+        )
+        attn[pl.ds(0, tokens), at] = primal.astype(jnp.bfloat16)
+        attn[pl.ds(tokens, tokens), at] = tangent.astype(jnp.bfloat16)
     tm, h, f = (lax.axis_index(axis) for axis in ("tm", "height", "fsdp"))
     for piece, (units, rows) in zip(pieces, layout):
         for i, unit in enumerate(units):
@@ -184,84 +222,42 @@
                     start = start + ((tm & 3) ^ dq) * rows
                 start = pl.multiple_of(start, 16)
             weight[pl.ds(start, rows), :] = piece[pl.ds(i * rows, rows), :]
-    gap = jnp.zeros((inner, HD), jnp.bfloat16)
-    for head in range(p.shape[0]):
-        at = pl.ds(head * HD, HD)
-
-        def ordered(i):
-            halo = pl.ds(half + i * edge, edge)
-            base = tokens + i * half
-            return jnp.concatenate(
-                [
-                    own[pl.ds(base, edge), at],
-                    mids[pl.ds(i * inner, inner), at],
-                    own[pl.ds(base + edge, edge), at],
-                    par[pl.ds(base, half), at],
-                    near_a[halo, at],
-                    late_a[halo, at],
-                    gap,
-                    near_b[halo, at],
-                    late_b[halo, at],
-                ],
-                0,
-            )
-
-        values, values_t = ordered(0), ordered(1)
-        probs = p[head]
-        total[pl.ds(0, tokens), at] = jnp.dot(probs, values, preferred_element_type=jnp.float32)
-        total[pl.ds(tokens, tokens), at] = jnp.dot(
-            jnp.concatenate([w[head], probs], 1),
-            jnp.concatenate([values, values_t], 0),
-            preferred_element_type=jnp.float32,
-        )
-
-
-def values_known(probs, weights_t, values, pieces, layout, dout):
-    tokens, features = probs.shape[1], values[0].shape[1]
-    arrays = (probs, weights_t, *values, *pieces)
-    return pl.pallas_call(
-        lambda *refs: values_kernel(layout, *refs),
-        out_shape=(
-            jax.ShapeDtypeStruct((2 * tokens, features), jnp.float32),
-            jax.ShapeDtypeStruct((dout, features), jnp.bfloat16),
-        ),
-        in_specs=[pl.BlockSpec(memory_space=pltpu.VMEM)] * len(arrays),
-        out_specs=[pl.BlockSpec(memory_space=pltpu.VMEM)] * 2,
-        compiler_params=pltpu.CompilerParams(vmem_limit_bytes=VMEM_LIMIT),
-        cost_estimate=SMALL,
-        name="values",
-    )(*arrays)
-
-
-def project_kernel(gate, slope, mid, total, weight, v_mid, out_p, out_t, attn):
-    tokens = out_p.shape[0]
-    for head in range(mid.shape[0]):
-        at = pl.ds(head * HD, HD)
-        rest = jnp.dot(mid[head], v_mid[:, at], preferred_element_type=jnp.float32)
-        attn[:, at] = (total[:, at] + rest).astype(jnp.bfloat16)
     width = 256
-    for first in range(0, weight.shape[0], width):
+    copies = []
+    for step, first in enumerate(range(0, weight.shape[0], width)):
         cols = pl.ds(first, width)
         both = dot_nt(attn[...], weight[cols, :])
         main, main_t = both[:tokens], both[tokens:]
         gate_row, slope_row = gate[:, cols], slope[:, cols]
-        out_p[:, cols] = (gate_row * main).astype(jnp.bfloat16)
-        out_t[:, cols] = (gate_row * main_t + slope_row * main).astype(jnp.bfloat16)
-
-
-def project(gate, slope, mid, total, weight, v_mid):
-    rows, features = total.shape
-    dout = weight.shape[0]
-    out = jax.ShapeDtypeStruct((rows // 2, dout), jnp.bfloat16)
+        rounded[0, :, cols] = (gate_row * main).astype(jnp.bfloat16)
+        rounded[1, :, cols] = (gate_row * main_t + slope_row * main).astype(jnp.bfloat16)
+        for i, out in enumerate((out_p, out_t)):
+            copies.append(pltpu.make_async_copy(rounded.at[i, :, cols], out.at[:, cols], sems.at[step, i]))
+            copies[-1].start()
+    for copy in copies:
+        copy.wait()
+
+
+def finish(gate, slope, probs, weights_t, values, pieces, layout):
+    tokens, features = probs.shape[1], values[0].shape[1]
+    dout = gate.shape[1]
+    arrays = (gate, slope, probs, weights_t, *values, *pieces)
+    out = jax.ShapeDtypeStruct((tokens, dout), jnp.bfloat16)
     return pl.pallas_call(
-        project_kernel,
+        lambda *refs: finish_kernel(layout, *refs),
         out_shape=(out, out),
-        in_specs=[pl.BlockSpec(memory_space=pltpu.VMEM)] * 6,
-        scratch_shapes=[pltpu.VMEM((rows, features), jnp.bfloat16)],
+        in_specs=[pl.BlockSpec(memory_space=pltpu.VMEM)] * len(arrays),
+        out_specs=[pl.BlockSpec(memory_space=pl.ANY)] * 2,
+        scratch_shapes=[
+            pltpu.VMEM((dout, features), jnp.bfloat16),
+            pltpu.VMEM((2 * tokens, features), jnp.bfloat16),
+            pltpu.VMEM((2, tokens, dout), jnp.bfloat16),
+            pltpu.SemaphoreType.DMA((dout // 256, 2)),
+        ],
         compiler_params=pltpu.CompilerParams(vmem_limit_bytes=VMEM_LIMIT),
         cost_estimate=SMALL,
-        name="project",
-    )(gate, slope, mid, total, weight, v_mid)
+        name="finish",
+    )(*arrays)
 
 
 def local(
@@ -321,10 +317,10 @@
         "par": (("own_parts",), lambda parts: swap(parts[0], "height", 1)),
         "v_mid": (("own_parts",), lambda parts: swap(parts[1], "height", 1)),
         "near_a": (("own_parts",), lambda parts: swap(parts[2], "tm", 1)),
-        "near_b": (("own_parts",), lambda parts: swap_odd(parts[3], "tm")),
+        "near_b": (("own_parts",), lambda parts: swap_odd_alone(parts[3], "tm")),
         "late_parts": (("k_par", "par"), late_parts),
         "late_a": (("late_parts",), lambda sides: swap(sides[0], "tm", 1)),
-        "late_b": (("late_parts",), lambda sides: swap_odd(sides[1], "tm")),
+        "late_b": (("late_parts",), lambda sides: swap_odd(sides[1], False)),
         "scores": (
             ("k_par", "par", "near_a", "near_b", "late_a", "late_b"),
             lambda *arrays: scores(q, qt, k, kt, *arrays),
@@ -343,13 +339,13 @@
         steps["half"] = (("pair",), lambda pair: cat(quarter(mine ^ 2), pair))
         steps["twos"] = (("pair",), lambda pair: swap(pair, "fsdp", 2))
         steps["ones"] = (("half",), lambda half: swap(half, "fsdp", 1))
-        steps["threes"] = (("twos",), lambda twos: swap(twos, "fsdp", 1))
+        steps["threes"] = (("twos", "other_x"), lambda *units: swap(cat(*units), "fsdp", 1))
         steps["other_x"] = (("other",), lambda other: swap(other, "tm", 2))
-        steps["cross"] = (("ones", "twos"), lambda ones, twos: swap(cat(ones[2 * part :], twos), "tm", 2))
-        steps["cross_threes"] = (("threes",), lambda threes: swap(threes, "tm", 2))
+        steps["cross"] = (("twos",), lambda twos: swap(twos, "tm", 2))
+        steps["cross_threes"] = (("threes",), lambda threes: swap(threes[: 2 * part], "tm", 2))
         steps["mine"] = (("other", "ones", "twos", "threes", "other_x", "cross", "cross_threes"), cat)
-        units = [(1, 0, 0), (0, 1, 2), (0, 1, 0), (1, 1, 0), (0, 2, 0), (1, 2, 0), (0, 3, 0), (1, 3, 0)]
-        units += [(1, 0, 2), (1, 1, 2), (0, 2, 2), (1, 2, 2), (0, 3, 2), (1, 3, 2)]
+        units = [(1, 0, 0), (0, 1, 2), (0, 1, 0), (1, 1, 0), (0, 2, 0), (1, 2, 0), (0, 3, 0), (1, 3, 0), (1, 1, 2)]
+        units += [(1, 0, 2), (0, 2, 2), (1, 2, 2), (0, 3, 2), (1, 3, 2)]
         steps["near"] = (("mine",), lambda mine: swap(mine, "tm", 1))
         pieces = ("mine", "near")
         layout = [([(0, 0, None)], wide), (units, part), (near(units), part)]
@@ -369,12 +365,11 @@
             known[name] = make(*arrays)
         return known[name]
 
-    probs, weights_t, mid = get("scores")
+    probs, weights_t = get("scores")
     own, middle, _, _ = get("own_parts")
-    known_values = (own, middle, *(get(name) for name in ("par", "near_a", "near_b", "late_a", "late_b")))
+    values = (own, middle, *(get(name) for name in ("par", "near_a", "near_b", "late_a", "late_b", "v_mid")))
     parts = ([block] if in_quarters else []) + [get(piece) for piece in pieces]
-    total, weight = values_known(probs, weights_t, known_values, parts, layout, gate_table.shape[1])
-    out_p, out_t = project(*get("gates"), mid, total, weight, get("v_mid"))
+    out_p, out_t = finish(*get("gates"), probs, weights_t, values, parts, layout)
     shape = query_primal.shape[:-1] + (out_p.shape[1],)
     return out_p.reshape(shape), out_t.reshape(shape)
 

time: 60.1 us -> 54.7 us (0.910)
  waiting for transfers between devices: 24.3 us -> 12.5 us
  starting transfers between devices: 22.1 us -> 29.9 us
  Pallas kernels: 10.6 us -> 9.25 us
    ppermute x13, waiting for transfers between devices: 21.5 us -> 9.48 us  [swap(): return lax.ppermute(value, axis, pairs)]
    ppermute x13, starting transfers between devices: 14.2 us -> 23.6 us  [swap(): return lax.ppermute(value, axis, pairs)]
    ppermute x2, starting transfers between devices: 7.9 us -> 6.29 us  [the longest x1 6.07 us: swap_odd_alone(): return lax.ppermute(value, axis, pairs)]
    pallas_call x3 -> x2, Pallas kernels: 6.49 us -> 5.2 us  [the longest x1 3.42 us: finish(): pl.pallas_call(lambda *refs: finish_kernel(layout, *refs), out_shape=(out...]
where the time goes in v3:
time: 54.7 us; the launch traced here: 54.5 us
  starting transfers between devices  29.9 us (55%)
  waiting for transfers between devices  12.5 us (23%)
  Pallas kernels  9.25 us (17%)
  between operations  1.57 us (3%)
  local copies, waits for them, and re-layouts  1.23 us (2%)
    ppermute x13, starting transfers between devices, swap(): return lax.ppermute(value, axis, pairs)  23.6 us
    ppermute x13, waiting for transfers between devices, swap(): return lax.ppermute(value, axis, pairs)  9.48 us
    ppermute x1, starting transfers between devices, swap_odd_alone(): return lax.ppermute(value, axis, pairs)  6.07 us
    pallas_call x2, Pallas kernels, gather_rows(): pl.pallas_call(kernel, out_shape=[jax.ShapeDtypeStruct((n, features), sou...  4.04 us
    pallas_call x1, Pallas kernels, finish(): pl.pallas_call(lambda *refs: finish_kernel(layout, *refs), out_shape=(out...  3.42 us
    pallas_call x1, Pallas kernels, scores(): pl.pallas_call(score_kernel, out_shape=(out, out), in_specs=[pl.BlockSpec...  1.78 us
    ppermute x1, waiting for transfers between devices, swap_odd(): return lax.ppermute(value, ('tm', 'fsdp'), pairs)  1.6 us
    ppermute x1, waiting for transfers between devices, swap_odd_alone(): return lax.ppermute(value, axis, pairs)  1.39 us
  transfers between devices with their start and end apart: 15, of which 6 were waited for; matrix products, arithmetic and copies ran while one was open for 0% of the time, Pallas kernels for 11%

profile of v3, /device:TPU:1, one launch (start us, length us, event | category | flops | bytes accessed | tf_op | source)
XLA Modules:
  0.0 54.5 jit_solution(6456646863205671460)
XLA Ops:
  0.6 1.0 %dynamic-slice_bitcast_fusion = (bf16[48,1536]{1,0:T(8,128)(2,1)S(1)}, bf16[48,1536]{1,0:T(8,128)(2,1)S(1)}) fusion(bf16[1536,192]{0,1:T(8,128)(2,1)} %param.16, s32[]{:T(128)S(6)} %select_n.7, s32[]{:T(128)S(6)} %select_n.6), kind=kLoop, calls=%fused_computation.3 | loop fusion | bytes 589832 | tf_op jit(solution)/shard_map/dynamic_slice | solution.py:333
  1.6 2.1 %collective-permute-start = (bf16[48,1536]{1,0:T(8,128)(2,1)S(1)}, bf16[48,1536]{1,0:T(8,128)(2,1)S(1)}, u32[]{:S(2)}, u32[]{:S(2)}) collective-permute-start(bf16[48,1536]{1,0:T(8,128)(2,1)S(1)} %get-tuple-element.53), channel_id=1, source_target_pairs={{0,4},{4,0},{1,5},{5,1},{2,6},{6,2},{3,7},{7,3},{8,12},{12,8},{9,1... | collective-permute-start | bytes 442376 | tf_op jit(solution)/shard_map/ppermute | solution.py:30
  3.9 3.0 %own_parts.1 = (bf16[256,1536]{1,0:T(8,128)(2,1)}, bf16[128,1536]{1,0:T(8,128)(2,1)}, bf16[128,1536]{1,0:T(8,128)(2,1)}, bf16[128,1536]{1,0:T(8,128)(2,1)}) custom-call(bf16[128,1536]{1,0:T(8,128)(2,1)} %bitcast.15, bf16[128,1536]{1,0:T(8,128)(2,1)} %bitcast.17, bf16[128,1536]{1,0:T(8,128)(2,1)} %bitcast.21, bf16[128,1536]{1,0:T(8,128)(2,1)} %bitcast.22), custom_call_target="tpu_custom_call" | custom-call | flops 1 | bytes 1 | tf_op jit(solution)/shard_map/own_parts/pallas_call | solution.py:81
  6.8 1.5 %collective-permute-start.3 = (bf16[256,1536]{1,0:T(8,128)(2,1)}, bf16[256,1536]{1,0:T(8,128)(2,1)S(1)}, u32[]{:S(2)}, u32[]{:S(2)}) collective-permute-start(bf16[256,1536]{1,0:T(8,128)(2,1)} %get-tuple-element.27.refs_4_), channel_id=1, source_target_pairs={{0,4},{4,0},{1,5},{5,1},{2,6},{6,2},{3,7},{7,3},{8,12},{12,8},{9,1... | collective-permute-start | bytes 2359304 | tf_op jit(solution)/shard_map/ppermute | solution.py:30
  8.3 2.4 %collective-permute-start.1 = (bf16[96,1536]{1,0:T(8,128)(2,1)S(1)}, bf16[96,1536]{1,0:T(8,128)(2,1)S(1)}, u32[]{:S(2)}, u32[]{:S(2)}) collective-permute-start(bf16[96,1536]{1,0:T(8,128)(2,1)S(1)} %pad_maximum_fusion.2), channel_id=1, source_target_pairs={{0,2},{1,3},{2,0},{3,1},{4,6},{5,7},{6,4},{7,5},{8,10},{9,11},{10,... | collective-permute-start | bytes 884744 | tf_op jit(solution)/shard_map/ppermute | solution.py:30
  10.7 1.4 %collective-permute-start.11 = (bf16[144,1536]{1,0:T(8,128)(2,1)S(1)}, bf16[144,1536]{1,0:T(8,128)(2,1)S(1)}, u32[]{:S(2)}, u32[]{:S(2)}) collective-permute-start(bf16[144,1536]{1,0:T(8,128)(2,1)S(1)} %pad_maximum_fusion.1), channel_id=1, source_target_pairs={{0,1},{1,0},{2,3},{3,2},{4,5},{5,4},{6,7},{7,6},{8,9},{9,8},{10,11... | collective-permute-start | bytes 1327112 | tf_op jit(solution)/shard_map/ppermute | solution.py:30
  12.1 1.2 %collective-permute-start.4 = (bf16[48,1536]{1,0:T(8,128)(2,1)S(1)}, bf16[48,1536]{1,0:T(8,128)(2,1)S(1)}, u32[]{:S(2)}, u32[]{:S(2)}) collective-permute-start(bf16[48,1536]{1,0:T(8,128)(2,1)S(1)} %collective-permute-done), channel_id=1, source_target_pairs={{0,16},{8,24},{16,0},{24,8},{1,17},{9,25},{17,1},{25,9},{2,18},{10... | collective-permute-start | bytes 442376 | tf_op jit(solution)/shard_map/ppermute | solution.py:30
  13.3 3.1 %collective-permute-done.4 = bf16[48,1536]{1,0:T(8,128)(2,1)S(1)} collective-permute-done((bf16[48,1536]{1,0:T(8,128)(2,1)S(1)}, bf16[48,1536]{1,0:T(8,128)(2,1)S(1)}, u32[]{:S(2)}, u32[]{:S(2)}) %collective-permute-start.4) | collective-permute-done | bytes 147488 | tf_op jit(solution)/shard_map/ppermute | solution.py:30
  16.4 6.1 %collective-permute-start.5 = (bf16[128,1536]{1,0:T(8,128)(2,1)}, bf16[128,1536]{1,0:T(8,128)(2,1)S(1)}, u32[]{:S(2)}, u32[]{:S(2)}) collective-permute-start(bf16[128,1536]{1,0:T(8,128)(2,1)} %get-tuple-element.38), channel_id=1, source_target_pairs={{8,16},{16,8},{9,17},{17,9},{10,18},{18,10},{11,19},{19,11},{12,20... | collective-permute-start | bytes 1179656 | tf_op jit(solution)/shard_map/ppermute | solution.py:50
  22.5 1.3 %collective-permute-start.10 = (bf16[128,1536]{1,0:T(8,128)(2,1)}, bf16[128,1536]{1,0:T(8,128)(2,1)S(1)}, u32[]{:S(2)}, u32[]{:S(2)}) collective-permute-start(bf16[128,1536]{1,0:T(8,128)(2,1)} %get-tuple-element.48.refs_5_), channel_id=1, source_target_pairs={{0,4},{4,0},{1,5},{5,1},{2,6},{6,2},{3,7},{7,3},{8,12},{12,8},{9,1... | collective-permute-start | bytes 1179656 | tf_op jit(solution)/shard_map/ppermute | solution.py:30
  23.8 1.3 %collective-permute-start.7 = (bf16[144,1536]{1,0:T(8,128)(2,1)S(1)}, bf16[144,1536]{1,0:T(8,128)(2,1)S(1)}, u32[]{:S(2)}, u32[]{:S(2)}) collective-permute-start(bf16[144,1536]{1,0:T(8,128)(2,1)S(1)} %pad_maximum_fusion), channel_id=1, source_target_pairs={{0,1},{1,0},{2,3},{3,2},{4,5},{5,4},{6,7},{7,6},{8,9},{9,8},{10,11... | collective-permute-start | bytes 1327112 | tf_op jit(solution)/shard_map/ppermute | solution.py:30
  25.1 0.6 %collective-permute-done.11 = bf16[144,1536]{1,0:T(8,128)(2,1)S(1)} collective-permute-done((bf16[144,1536]{1,0:T(8,128)(2,1)S(1)}, bf16[144,1536]{1,0:T(8,128)(2,1)S(1)}, u32[]{:S(2)}, u32[]{:S(2)}) %collective-permute-start.11) | collective-permute-done | bytes 442400 | tf_op jit(solution)/shard_map/ppermute | solution.py:30
  25.7 1.2 %collective-permute-start.12 = (bf16[96,1536]{1,0:T(8,128)(2,1)S(1)}, bf16[96,1536]{1,0:T(8,128)(2,1)S(1)}, u32[]{:S(2)}, u32[]{:S(2)}) collective-permute-start(bf16[96,1536]{1,0:T(8,128)(2,1)S(1)} %collective-permute-done.1), channel_id=1, source_target_pairs={{0,16},{8,24},{16,0},{24,8},{1,17},{9,25},{17,1},{25,9},{2,18},{10... | collective-permute-start | bytes 884744 | tf_op jit(solution)/shard_map/ppermute | solution.py:30
  27.0 1.4 %collective-permute-done.5.near_b.refs_8_ = bf16[128,1536]{1,0:T(8,128)(2,1)S(1)} collective-permute-done((bf16[128,1536]{1,0:T(8,128)(2,1)}, bf16[128,1536]{1,0:T(8,128)(2,1)S(1)}, u32[]{:S(2)}, u32[]{:S(2)}) %collective-permute-start.5) | collective-permute-done | bytes 393248 | tf_op jit(solution)/shard_map/ppermute | solution.py:50
  28.4 3.6 %collective-permute-start.6 = (bf16[128,1536]{1,0:T(8,128)(2,1)S(1)}, bf16[128,1536]{1,0:T(8,128)(2,1)S(1)}, u32[]{:S(2)}, u32[]{:S(2)}) collective-permute-start(bf16[128,1536]{1,0:T(8,128)(2,1)S(1)} %copy-done.9), channel_id=1, source_target_pairs={{0,8},{8,0},{16,24},{24,16},{1,9},{9,1},{17,25},{25,17},{2,10},{10... | collective-permute-start | bytes 1179656 | tf_op jit(solution)/shard_map/ppermute | solution.py:30
  32.0 4.1 %collective-permute-done.7 = bf16[144,1536]{1,0:T(8,128)(2,1)S(1)} collective-permute-done((bf16[144,1536]{1,0:T(8,128)(2,1)S(1)}, bf16[144,1536]{1,0:T(8,128)(2,1)S(1)}, u32[]{:S(2)}, u32[]{:S(2)}) %collective-permute-start.7) | collective-permute-done | bytes 442400 | tf_op jit(solution)/shard_map/ppermute | solution.py:30
  36.2 1.0 %collective-permute-start.13 = (bf16[96,1536]{1,0:T(8,128)(2,1)S(1)}, bf16[96,1536]{1,0:T(8,128)(2,1)S(1)}, u32[]{:S(2)}, u32[]{:S(2)}) collective-permute-start(bf16[96,1536]{1,0:T(8,128)(2,1)S(1)} %slice.4), channel_id=1, source_target_pairs={{0,16},{8,24},{16,0},{24,8},{1,17},{9,25},{17,1},{25,9},{2,18},{10... | collective-permute-start | bytes 884744 | tf_op jit(solution)/shard_map/ppermute | solution.py:30
  37.2 1.1 %late_parts.1 = (bf16[128,1536]{1,0:T(8,128)(2,1)S(1)}, bf16[128,1536]{1,0:T(8,128)(2,1)S(1)}) custom-call(bf16[128,1536]{1,0:T(8,128)(2,1)S(1)} %collective-permute-done.2.refs_0_.k_par, bf16[256,1536]{1,0:T(8,128)(2,1)S(1)} %collective-permute-done.3.refs_1_.par.refs_6_), custom_call_target="tpu_custom_call" | custom-call | flops 1 | bytes 1 | tf_op jit(solution)/shard_map/late_parts/pallas_call | solution.py:81
  38.3 2.5 %collective-permute-start.8 = (bf16[128,1536]{1,0:T(8,128)(2,1)S(1)}, bf16[128,1536]{1,0:T(8,128)(2,1)S(1)}, u32[]{:S(2)}, u32[]{:S(2)}) collective-permute-start(bf16[128,1536]{1,0:T(8,128)(2,1)S(1)} %get-tuple-element.44), channel_id=1, source_target_pairs={{0,8},{8,0},{16,24},{24,16},{1,9},{9,1},{17,25},{25,17},{2,10},{10... | collective-permute-start | bytes 1179656 | tf_op jit(solution)/shard_map/ppermute | solution.py:30
  41.2 1.7 %collective-permute-done.13 = bf16[96,1536]{1,0:T(8,128)(2,1)S(1)} collective-permute-done((bf16[96,1536]{1,0:T(8,128)(2,1)S(1)}, bf16[96,1536]{1,0:T(8,128)(2,1)S(1)}, u32[]{:S(2)}, u32[]{:S(2)}) %collective-permute-start.13) | collective-permute-done | bytes 294944 | tf_op jit(solution)/shard_map/ppermute | solution.py:30
  42.9 4.0 %collective-permute-start.14 = (bf16[672,1536]{1,0:T(8,128)(2,1)S(1)}, bf16[672,1536]{1,0:T(8,128)(2,1)S(1)}, u32[]{:S(2)}, u32[]{:S(2)}) collective-permute-start(bf16[672,1536]{1,0:T(8,128)(2,1)S(1)} %constant_dynamic-update-slice_fusion.refs_13_), channel_id=1, source_target_pairs={{0,8},{8,0},{16,24},{24,16},{1,9},{9,1},{17,25},{25,17},{2,10},{10... | collective-permute-start | bytes 6193160 | tf_op jit(solution)/shard_map/ppermute | solution.py:30
  47.6 1.6 %collective-permute-done.9.late_b.refs_10_ = bf16[128,1536]{1,0:T(8,128)(2,1)S(1)} collective-permute-done((bf16[128,1536]{1,0:T(8,128)(2,1)S(1)}, bf16[128,1536]{1,0:T(8,128)(2,1)S(1)}, u32[]{:S(2)}, u32[]{:S(2)}) %collective-permute-start.9) | collective-permute-done | bytes 393248 | tf_op jit(solution)/shard_map/ppermute | solution.py:43
  49.3 1.8 %scores.1 = (bf16[12,128,384]{2,1,0:T(8,128)(2,1)S(1)}, bf16[12,128,384]{2,1,0:T(8,128)(2,1)S(1)}) custom-call(bf16[128,1536]{1,0:T(8,128)(2,1)S(1)} %bitcast.19, bf16[128,1536]{1,0:T(8,128)(2,1)S(1)} %bitcast.20, bf16[128,1536]{1,0:T(8,128)(2,1)S(1)} %bitcast.16, bf16[128,1536]{1,0:T(8,128)(2,1)S(1)} %bitcast.18, ...), custom_call_target="tpu_custom_call" | custom-call | flops 20000000000 | bytes 1 | tf_op jit(solution)/shard_map/scores/pallas_call | solution.py:165
  51.1 3.4 %finish.1 = (bf16[128,1536]{1,0:T(8,128)(2,1)}, bf16[128,1536]{1,0:T(8,128)(2,1)}) custom-call(f32[1,1536]{1,0:T(1,128)S(1)} %get-tuple-element.35.refs_0_, f32[1,1536]{1,0:T(1,128)S(1)} %get-tuple-element.36.refs_1_, bf16[12,128,384]{2,1,0:T(8,128)(2,1)S(1)} %get-tuple-element.46.refs_2_, bf16[12,128,384]{2,1,0:T(8,128)(2,1)S(1)} %get-tuple-element.47.refs_3_, ...), custom_call_target="tpu_custom_call" | custom-call | flops 1 | bytes 1 | tf_op jit(solution)/shard_map/finish/pallas_call | solution.py:246
  (43 shorter events, 0.6 us)
Async XLA Ops:
  1.6 6.6 %collective-permute-start = (bf16[48,1536]{1,0:T(8,128)(2,1)S(1)}, bf16[48,1536]{1,0:T(8,128)(2,1)S(1)}, u32[]{:S(2)}, u32[]{:S(2)}) collective-permute-start(bf16[48,1536]{1,0:T(8,128)(2,1)S(1)} %get-tuple-element.53), channel_id=1, source_target_pairs={{0,4},{4,0},{1,5},{5,1},{2,6},{6,2},{3,7},{7,3},{8,12},{12,8},{9,1... | collective-permute-start | bytes 442376 | tf_op jit(solution)/shard_map/ppermute | solution.py:30
  3.8 18.7 %collective-permute-start.2 = (bf16[128,1536]{1,0:T(8,128)(2,1)}, bf16[128,1536]{1,0:T(8,128)(2,1)S(1)}, u32[]{:S(2)}, u32[]{:S(2)}) collective-permute-start(bf16[128,1536]{1,0:T(8,128)(2,1)} %bitcast.14), channel_id=1, source_target_pairs={{0,4},{4,0},{1,5},{5,1},{2,6},{6,2},{3,7},{7,3},{8,12},{12,8},{9,1... | collective-permute-start | bytes 1179656 | tf_op jit(solution)/shard_map/ppermute | solution.py:30
  6.8 21.6 %copy-start.9 = (bf16[128,1536]{1,0:T(8,128)(2,1)S(1)}, bf16[128,1536]{1,0:T(8,128)(2,1)}, u32[]{:S(2)}) copy-start(bf16[128,1536]{1,0:T(8,128)(2,1)} %get-tuple-element.39) | copy-start | bytes 1179652
  6.8 30.4 %collective-permute-start.3 = (bf16[256,1536]{1,0:T(8,128)(2,1)}, bf16[256,1536]{1,0:T(8,128)(2,1)S(1)}, u32[]{:S(2)}, u32[]{:S(2)}) collective-permute-start(bf16[256,1536]{1,0:T(8,128)(2,1)} %get-tuple-element.27.refs_4_), channel_id=1, source_target_pairs={{0,4},{4,0},{1,5},{5,1},{2,6},{6,2},{3,7},{7,3},{8,12},{12,8},{9,1... | collective-permute-start | bytes 2359304 | tf_op jit(solution)/shard_map/ppermute | solution.py:30
  8.3 15.5 %collective-permute-start.1 = (bf16[96,1536]{1,0:T(8,128)(2,1)S(1)}, bf16[96,1536]{1,0:T(8,128)(2,1)S(1)}, u32[]{:S(2)}, u32[]{:S(2)}) collective-permute-start(bf16[96,1536]{1,0:T(8,128)(2,1)S(1)} %pad_maximum_fusion.2), channel_id=1, source_target_pairs={{0,2},{1,3},{2,0},{3,1},{4,6},{5,7},{6,4},{7,5},{8,10},{9,11},{10,... | collective-permute-start | bytes 884744 | tf_op jit(solution)/shard_map/ppermute | solution.py:30
  10.7 15.0 %collective-permute-start.11 = (bf16[144,1536]{1,0:T(8,128)(2,1)S(1)}, bf16[144,1536]{1,0:T(8,128)(2,1)S(1)}, u32[]{:S(2)}, u32[]{:S(2)}) collective-permute-start(bf16[144,1536]{1,0:T(8,128)(2,1)S(1)} %pad_maximum_fusion.1), channel_id=1, source_target_pairs={{0,1},{1,0},{2,3},{3,2},{4,5},{5,4},{6,7},{7,6},{8,9},{9,8},{10,11... | collective-permute-start | bytes 1327112 | tf_op jit(solution)/shard_map/ppermute | solution.py:30
  12.1 4.3 %collective-permute-start.4 = (bf16[48,1536]{1,0:T(8,128)(2,1)S(1)}, bf16[48,1536]{1,0:T(8,128)(2,1)S(1)}, u32[]{:S(2)}, u32[]{:S(2)}) collective-permute-start(bf16[48,1536]{1,0:T(8,128)(2,1)S(1)} %collective-permute-done), channel_id=1, source_target_pairs={{0,16},{8,24},{16,0},{24,8},{1,17},{9,25},{17,1},{25,9},{2,18},{10... | collective-permute-start | bytes 442376 | tf_op jit(solution)/shard_map/ppermute | solution.py:30
  16.4 12.0 %collective-permute-start.5 = (bf16[128,1536]{1,0:T(8,128)(2,1)}, bf16[128,1536]{1,0:T(8,128)(2,1)S(1)}, u32[]{:S(2)}, u32[]{:S(2)}) collective-permute-start(bf16[128,1536]{1,0:T(8,128)(2,1)} %get-tuple-element.38), channel_id=1, source_target_pairs={{8,16},{16,8},{9,17},{17,9},{10,18},{18,10},{11,19},{19,11},{12,20... | collective-permute-start | bytes 1179656 | tf_op jit(solution)/shard_map/ppermute | solution.py:50
  22.5 20.4 %collective-permute-start.10 = (bf16[128,1536]{1,0:T(8,128)(2,1)}, bf16[128,1536]{1,0:T(8,128)(2,1)S(1)}, u32[]{:S(2)}, u32[]{:S(2)}) collective-permute-start(bf16[128,1536]{1,0:T(8,128)(2,1)} %get-tuple-element.48.refs_5_), channel_id=1, source_target_pairs={{0,4},{4,0},{1,5},{5,1},{2,6},{6,2},{3,7},{7,3},{8,12},{12,8},{9,1... | collective-permute-start | bytes 1179656 | tf_op jit(solution)/shard_map/ppermute | solution.py:30
  23.8 12.3 %collective-permute-start.7 = (bf16[144,1536]{1,0:T(8,128)(2,1)S(1)}, bf16[144,1536]{1,0:T(8,128)(2,1)S(1)}, u32[]{:S(2)}, u32[]{:S(2)}) collective-permute-start(bf16[144,1536]{1,0:T(8,128)(2,1)S(1)} %pad_maximum_fusion), channel_id=1, source_target_pairs={{0,1},{1,0},{2,3},{3,2},{4,5},{5,4},{6,7},{7,6},{8,9},{9,8},{10,11... | collective-permute-start | bytes 1327112 | tf_op jit(solution)/shard_map/ppermute | solution.py:30
  25.7 15.2 %collective-permute-start.12 = (bf16[96,1536]{1,0:T(8,128)(2,1)S(1)}, bf16[96,1536]{1,0:T(8,128)(2,1)S(1)}, u32[]{:S(2)}, u32[]{:S(2)}) collective-permute-start(bf16[96,1536]{1,0:T(8,128)(2,1)S(1)} %collective-permute-done.1), channel_id=1, source_target_pairs={{0,16},{8,24},{16,0},{24,8},{1,17},{9,25},{17,1},{25,9},{2,18},{10... | collective-permute-start | bytes 884744 | tf_op jit(solution)/shard_map/ppermute | solution.py:30
  27.0 20.6 %copy-start.3 = (f32[64,1536]{1,0:T(8,128)S(1)}, f32[64,1536]{1,0:T(8,128)}, u32[]{:S(2)}) copy-start(f32[64,1536]{1,0:T(8,128)} %gate) | copy-start | bytes 1179652
  27.0 20.6 %copy-start.4 = (f32[64,1536]{1,0:T(8,128)S(1)}, f32[64,1536]{1,0:T(8,128)}, u32[]{:S(2)}) copy-start(f32[64,1536]{1,0:T(8,128)} %slope) | copy-start | bytes 1179652
  28.4 19.2 %collective-permute-start.6 = (bf16[128,1536]{1,0:T(8,128)(2,1)S(1)}, bf16[128,1536]{1,0:T(8,128)(2,1)S(1)}, u32[]{:S(2)}, u32[]{:S(2)}) collective-permute-start(bf16[128,1536]{1,0:T(8,128)(2,1)S(1)} %copy-done.9), channel_id=1, source_target_pairs={{0,8},{8,0},{16,24},{24,16},{1,9},{9,1},{17,25},{25,17},{2,10},{10... | collective-permute-start | bytes 1179656 | tf_op jit(solution)/shard_map/ppermute | solution.py:30
  36.1 13.1 %copy-start.5 = (bf16[1,4,4,8,1536]{4,3,2,1,0:T(8,128)(2,1)S(1)}, bf16[1,4,4,8,1536]{4,3,2,1,0:T(8,128)(2,1)}, u32[]{:S(2)}) copy-start(bf16[1,4,4,8,1536]{4,3,2,1,0:T(8,128)(2,1)} %param.11) | copy-start | bytes 1179652
  36.2 13.1 %copy-start.6 = (bf16[1,4,4,8,1536]{4,3,2,1,0:T(8,128)(2,1)S(1)}, bf16[1,4,4,8,1536]{4,3,2,1,0:T(8,128)(2,1)}, u32[]{:S(2)}) copy-start(bf16[1,4,4,8,1536]{4,3,2,1,0:T(8,128)(2,1)} %param.14) | copy-start | bytes 1179652
  36.2 13.0 %copy-start.7 = (bf16[1,4,4,8,1536]{4,3,2,1,0:T(8,128)(2,1)S(1)}, bf16[1,4,4,8,1536]{4,3,2,1,0:T(8,128)(2,1)}, u32[]{:S(2)}) copy-start(bf16[1,4,4,8,1536]{4,3,2,1,0:T(8,128)(2,1)} %param.10) | copy-start | bytes 1179652
  36.2 13.0 %copy-start.8 = (bf16[1,4,4,8,1536]{4,3,2,1,0:T(8,128)(2,1)S(1)}, bf16[1,4,4,8,1536]{4,3,2,1,0:T(8,128)(2,1)}, u32[]{:S(2)}) copy-start(bf16[1,4,4,8,1536]{4,3,2,1,0:T(8,128)(2,1)} %param.13) | copy-start | bytes 1179652
  36.2 6.6 %collective-permute-start.13 = (bf16[96,1536]{1,0:T(8,128)(2,1)S(1)}, bf16[96,1536]{1,0:T(8,128)(2,1)S(1)}, u32[]{:S(2)}, u32[]{:S(2)}) collective-permute-start(bf16[96,1536]{1,0:T(8,128)(2,1)S(1)} %slice.4), channel_id=1, source_target_pairs={{0,16},{8,24},{16,0},{24,8},{1,17},{9,25},{17,1},{25,9},{2,18},{10... | collective-permute-start | bytes 884744 | tf_op jit(solution)/shard_map/ppermute | solution.py:30
  38.3 9.3 %collective-permute-start.8 = (bf16[128,1536]{1,0:T(8,128)(2,1)S(1)}, bf16[128,1536]{1,0:T(8,128)(2,1)S(1)}, u32[]{:S(2)}, u32[]{:S(2)}) collective-permute-start(bf16[128,1536]{1,0:T(8,128)(2,1)S(1)} %get-tuple-element.44), channel_id=1, source_target_pairs={{0,8},{8,0},{16,24},{24,16},{1,9},{9,1},{17,25},{25,17},{2,10},{10... | collective-permute-start | bytes 1179656 | tf_op jit(solution)/shard_map/ppermute | solution.py:30
  40.9 8.3 %collective-permute-start.9 = (bf16[128,1536]{1,0:T(8,128)(2,1)S(1)}, bf16[128,1536]{1,0:T(8,128)(2,1)S(1)}, u32[]{:S(2)}, u32[]{:S(2)}) collective-permute-start(bf16[128,1536]{1,0:T(8,128)(2,1)S(1)} %get-tuple-element.45), channel_id=1, source_target_pairs={{0,1},{1,0},{2,3},{3,2},{8,16},{9,17},{10,18},{11,19},{16,8},{17,9... | collective-permute-start | bytes 1179656 | tf_op jit(solution)/shard_map/ppermute | solution.py:43
  42.9 8.2 %collective-permute-start.14 = (bf16[672,1536]{1,0:T(8,128)(2,1)S(1)}, bf16[672,1536]{1,0:T(8,128)(2,1)S(1)}, u32[]{:S(2)}, u32[]{:S(2)}) collective-permute-start(bf16[672,1536]{1,0:T(8,128)(2,1)S(1)} %constant_dynamic-update-slice_fusion.refs_13_), channel_id=1, source_target_pairs={{0,8},{8,0},{16,24},{24,16},{1,9},{9,1},{17,25},{25,17},{2,10},{10... | collective-permute-start | bytes 6193160 | tf_op jit(solution)/shard_map/ppermute | solution.py:30
  49.2 1.8 %copy-start = (bf16[1536,192]{0,1:T(8,128)(2,1)S(1)}, bf16[1536,192]{0,1:T(8,128)(2,1)}, u32[]{:S(2)}) copy-start(bf16[1536,192]{0,1:T(8,128)(2,1)} %param.16) | copy-start | bytes 1769476
  49.2 1.8 %copy-start.1 = (bf16[256,1536]{1,0:T(8,128)(2,1)S(1)}, bf16[256,1536]{1,0:T(8,128)(2,1)}, u32[]{:S(2)}) copy-start(bf16[256,1536]{1,0:T(8,128)(2,1)} %get-tuple-element.27.refs_4_) | copy-start | bytes 2359300
  (1 other events, 1.8 us)
